TPU v7x, 128 devices: a whole 4x4x4 slice. The times are simulated.
128 devices in a mesh: dp: 4 (over y_hi, core), expert: 32 (over y_lo, x, z).
Axes of the slice: x: 4, y: 4 (y_hi: 2, y_lo: 2; y = y_hi * 2 + y_lo), z: 4, core: 2. Of those that a mesh axis runs over, the one named last changes fastest.
Arguments:
- tokens: bfloat16 [16384, 2048], P(('dp', 'expert')), may hold values from -6 to 6
- d_mixed: bfloat16 [16384, 2048], P(('dp', 'expert')), may hold values from -6 to 6
- w_in: bfloat16 [128, 2048, 768], P('expert'), may hold values from -0.125 to 0.125
- w_out: bfloat16 [128, 384, 2048], P('expert'), may hold values from -0.3125 to 0.3125
- expert_ids: int32 [16384, 8], P(('dp', 'expert')), may hold values from 0 to 127, all different within a row; in each aligned block of 128 rows (0 to 127, 128 to 255, ...) at most 10 rows name the same one
- gate_fixed: int32 [16384, 8], P(('dp', 'expert')), may hold values from 1 to 65535
- placement: int32 [128], replicated, may hold values from 0 to 127, each once
Outputs:
- mixed: bfloat16 [16384, 2048], P(('dp', 'expert'))
- d_tokens: bfloat16 [16384, 2048], P(('dp', 'expert'))
- grad_in: bfloat16 [128, 2048, 768], P('expert', 'dp')
- grad_out: bfloat16 [128, 384, 2048], P('expert', None, 'dp')
Inputs may be any that keep to these rules, and one draw needn't show every extreme that they name: `expert_ids`: each row names 8 different experts. Among the rows of one device no expert is named more than 10 times, and in every draw some expert is named exactly 10 times by the rows of some device. Each number appears once: expert e's weights are in slot placement[e], held by expert-axis index placement[e] // 4.
All inputs are finite; a program needn't handle non-finite values.
Results may differ from a plain program's by a relative error of at most 0.009.
Values may be sent and summed in bfloat16 or wider, within the bound.
A program may use at most 192 MiB of HBM per device.

v0:
```python
import jax
import jax.numpy as jnp
from jax import lax
from jax.sharding import PartitionSpec as P


def gather_routes(rows, position, scales):
    total = jnp.zeros((position.shape[0], rows.shape[1]), jnp.float32)
    for k in range(position.shape[1]):
        picked = jnp.take(rows, position[:, k], axis=0).astype(jnp.float32)
        total = total + scales[:, k : k + 1] * picked
    return total


def body(tokens, d_mixed, w_in, w_out, expert_ids, gate_fixed, placement):
    tok_rows, width = tokens.shape
    local_count = w_in.shape[0]
    hidden = w_out.shape[1]
    axis_count = lax.axis_size("expert")
    experts_all = local_count * axis_count
    top = expert_ids.shape[1]
    capacity = max(2, 5 * tok_rows * top // (4 * experts_all))
    slots = experts_all * capacity
    gates = gate_fixed.astype(jnp.float32)
    gates = gates / jnp.sum(gates, axis=1, keepdims=True)
    catalog = jnp.arange(experts_all, dtype=jnp.int32)
    slot_of = jnp.sum(jnp.where(expert_ids[:, :, None] == catalog, placement, 0), axis=2)
    flat_slot = slot_of.reshape(-1)
    onehot = (flat_slot[:, None] == catalog).astype(jnp.int32)
    rank = jnp.sum(jnp.cumsum(onehot, axis=0) * onehot, axis=1) - 1
    position = (flat_slot * capacity + rank).reshape(tok_rows, top)
    places = jnp.arange(slots, dtype=jnp.int32)
    match = position[:, :, None] == places
    dispatch = jnp.any(match, axis=1).astype(jnp.bfloat16)
    slot_gate = jnp.sum(jnp.where(match, gates[:, :, None], 0.0), axis=(0, 1))
    blocked = (axis_count, local_count, capacity, width)

    def to_slots(rows):
        return jnp.einsum("ts,td->sd", dispatch, rows, preferred_element_type=jnp.float32)

    x_send = to_slots(tokens).astype(jnp.bfloat16).reshape(blocked)
    x_recv = lax.all_to_all(x_send, "expert", split_axis=0, concat_axis=0, tiled=True)
    pre = jnp.einsum("secd,edf->secf", x_recv, w_in, preferred_element_type=jnp.float32)
    gate_part = pre[..., :hidden]
    up_part = pre[..., hidden:]
    sig = jax.nn.sigmoid(gate_part)
    silu = gate_part * sig
    act = (silu * up_part).astype(jnp.bfloat16)
    expert_out = jnp.einsum(
        "secf,efd->secd", act, w_out, preferred_element_type=jnp.float32
    ).astype(jnp.bfloat16)
    came_back = lax.all_to_all(
        expert_out, "expert", split_axis=0, concat_axis=0, tiled=True
    ).reshape(slots, width)
    mixed = gather_routes(came_back, position, gates).astype(jnp.bfloat16)
    d_recv = lax.all_to_all(
        (to_slots(d_mixed) * slot_gate[:, None]).astype(jnp.bfloat16).reshape(blocked),
        "expert",
        split_axis=0,
        concat_axis=0,
        tiled=True,
    )
    d_act = jnp.einsum("secd,efd->secf", d_recv, w_out, preferred_element_type=jnp.float32)
    d_gate = d_act * up_part * sig * (1.0 + gate_part * (1.0 - sig))
    d_up = d_act * silu
    d_pre = jnp.concatenate([d_gate, d_up], axis=3).astype(jnp.bfloat16)
    d_rows = jnp.einsum("secf,edf->secd", d_pre, w_in, preferred_element_type=jnp.float32).astype(
        jnp.bfloat16
    )
    returned = lax.all_to_all(d_rows, "expert", split_axis=0, concat_axis=0, tiled=True).reshape(
        slots, width
    )
    unit = jnp.ones((tok_rows, top), jnp.float32)
    d_tokens = gather_routes(returned, position, unit).astype(jnp.bfloat16)
    in_term = jnp.einsum("secd,secf->edf", x_recv, d_pre, preferred_element_type=jnp.float32)
    down_term = jnp.einsum("secf,secd->efd", act, d_recv, preferred_element_type=jnp.float32)
    summed_in, summed_out = (
        lax.psum_scatter(
            in_term.astype(jnp.bfloat16), "dp", scatter_dimension=1, tiled=True
        ).astype(jnp.float32),
        lax.psum_scatter(
            down_term.astype(jnp.bfloat16), "dp", scatter_dimension=2, tiled=True
        ).astype(jnp.float32),
    )
    grad_in = summed_in.astype(jnp.bfloat16)
    grad_out = summed_out.astype(jnp.bfloat16)
    return (mixed, d_tokens, grad_in, grad_out)


def solution(mesh):
    in_specs = (
        P(("dp", "expert"), None),
        P(("dp", "expert"), None),
        P("expert", None, None),
        P("expert", None, None),
        P(("dp", "expert"), None),
        P(("dp", "expert"), None),
        P(),
    )
    out_specs = (
        P(("dp", "expert"), None),
        P(("dp", "expert"), None),
        P("expert", "dp", None),
        P("expert", None, "dp"),
    )
    return jax.shard_map(body, mesh=mesh, in_specs=in_specs, out_specs=out_specs, check_vma=False)
```

profile of v0, /device:TPU:0, one launch (start us, length us, event | category | flops | bytes accessed | tf_op | source)
XLA Modules:
  0.0 543.7 jit_solution(6435203725975555539)
XLA Ops:
  17.9 9.5 %reshape.61 = bf16[32,4,10,2048]{3,2,1,0:T(8,128)(2,1)} reshape(bf16[1280,2048]{1,0:T(8,128)(2,1)} %convolution_convert_fusion) | data formatting | bytes 10485760 | tf_op jit(solution)/shard_map/reshape | solution.py:41
  27.4 10.7 %copy.59 = bf16[32,4,10,2048]{3,1,2,0:T(4,128)(2,1)} copy(bf16[32,4,10,2048]{3,2,1,0:T(8,128)(2,1)} %reshape.61) | data formatting | bytes 10485760 | tf_op jit(solution)/shard_map/reshape | solution.py:41
  38.1 9.5 %all-to-all-start = ((bf16[32,4,10,2048]{3,1,2,0:T(4,128)(2,1)}), bf16[32,4,10,2048]{3,1,2,0:T(4,128)(2,1)}, u32[]{:S(2)}, u32[]{:S(2)}) async-start(bf16[32,4,10,2048]{3,1,2,0:T(4,128)(2,1)} %copy.59), calls=%async_computation | async-start | bytes 10485760 | tf_op jit(solution)/shard_map/all_to_all | solution.py:42
  52.4 9.5 %reshape.63 = bf16[32,4,10,2048]{3,2,1,0:T(8,128)(2,1)} reshape(bf16[1280,2048]{1,0:T(8,128)(2,1)} %multiply_convert_fusion) | data formatting | bytes 10485760 | tf_op jit(solution)/shard_map/reshape | solution.py:57
  61.9 10.8 %copy.64 = bf16[32,4,10,2048]{3,1,2,0:T(4,128)(2,1)} copy(bf16[32,4,10,2048]{3,2,1,0:T(8,128)(2,1)} %reshape.63) | data formatting | bytes 10485760 | tf_op jit(solution)/shard_map/reshape | solution.py:57
  72.7 44.4 %all-to-all-done = bf16[32,4,10,2048]{3,1,2,0:T(4,128)(2,1)} async-done(((bf16[32,4,10,2048]{3,1,2,0:T(4,128)(2,1)}), bf16[32,4,10,2048]{3,1,2,0:T(4,128)(2,1)}, u32[]{:S(2)}, u32[]{:S(2)}) %all-to-all-start) | async-done | bytes 5242912 | tf_op jit(solution)/shard_map/all_to_all | solution.py:42
  117.1 8.9 %all-to-all-start.2 = ((bf16[32,4,10,2048]{3,1,2,0:T(4,128)(2,1)}), bf16[32,4,10,2048]{3,1,2,0:T(4,128)(2,1)}, u32[]{:S(2)}, u32[]{:S(2)}) async-start(bf16[32,4,10,2048]{3,1,2,0:T(4,128)(2,1)} %copy.64), calls=%async_computation.2 | async-start | bytes 10485760 | tf_op jit(solution)/shard_map/all_to_all | solution.py:56
  126.2 15.9 %fusion.17 = f32[32,4,10,768]{3,0,2,1:T(8,128)} fusion(bf16[4,2048,768]{2,1,0:T(8,128)(2,1)} %param.11, bf16[32,4,10,2048]{3,1,2,0:T(4,128)(2,1)} %all-to-all-done), kind=kOutput, calls=%fused_computation.37 | convolution fusion | flops 4026531840 | bytes 21757952 | tf_op jit(solution)/shard_map/secd,edf->secf/dot_general | solution.py:43
  142.1 53.3 %all-to-all-done.2 = bf16[32,4,10,2048]{3,1,2,0:T(4,128)(2,1)} async-done(((bf16[32,4,10,2048]{3,1,2,0:T(4,128)(2,1)}), bf16[32,4,10,2048]{3,1,2,0:T(4,128)(2,1)}, u32[]{:S(2)}, u32[]{:S(2)}) %all-to-all-start.2) | async-done | bytes 5242912 | tf_op jit(solution)/shard_map/all_to_all | solution.py:56
  195.4 12.8 %fusion.24 = (bf16[32,4,10,384]{3,0,2,1:T(8,128)(2,1)S(1)}, bf16[32,4,10,384]{3,0,2,1:T(8,128)(2,1)S(1)}, bf16[32,4,10,384]{3,0,2,1:T(8,128)(2,1)S(1)}) fusion(f32[32,4,10,768]{3,0,2,1:T(8,128)} %fusion.17, bf16[4,384,2048]{2,1,0:T(8,128)(2,1)} %param.12, bf16[32,4,10,2048]{3,1,2,0:T(4,128)(2,1)} %all-to-all-done.2), kind=kOutput, calls=%fused_computation.43 | convolution fusion | flops 2020638720 | bytes 18415616 | tf_op jit(solution)/shard_map/secd,efd->secf/dot_general | solution.py:63
  208.2 12.1 %bitcast_convert_fusion.1 = bf16[4,384,2048]{2,1,0:T(8,128)(2,1)} fusion(bf16[32,4,10,384]{3,0,2,1:T(8,128)(2,1)S(1)} %get-tuple-element.15, bf16[32,4,10,2048]{3,1,2,0:T(4,128)(2,1)} %all-to-all-done.2), kind=kOutput, calls=%fused_computation.17 | convolution fusion | flops 2016411648 | bytes 12517376 | tf_op jit(solution)/shard_map/secf,secd->efd/dot_general | solution.py:76
  220.8 28.8 %bitcast_convert_fusion = bf16[4,2048,768]{2,1,0:T(8,128)(2,1)} fusion(bf16[32,4,10,2048]{3,1,2,0:T(4,128)(2,1)} %all-to-all-done, bf16[32,4,10,384]{3,0,2,1:T(8,128)(2,1)S(1)} %get-tuple-element.14, bf16[32,4,10,384]{3,0,2,1:T(8,128)(2,1)S(1)} %get-tuple-element.13), kind=kOutput, calls=%fused_computation.16 | convolution fusion | flops 4036755456 | bytes 19791872 | tf_op jit(solution)/shard_map/secd,secf->edf/dot_general | solution.py:75
  249.6 6.1 %convert_bitcast_fusion.1 = bf16[32,4,10,2048]{3,0,2,1:T(8,128)(2,1)S(1)} fusion(bf16[32,4,10,384]{3,0,2,1:T(8,128)(2,1)S(1)} %get-tuple-element.15, bf16[4,384,2048]{2,1,0:T(8,128)(2,1)} %param.12), kind=kOutput, calls=%fused_computation.30 | convolution fusion | flops 2015887360 | bytes 12517376 | tf_op jit(solution)/shard_map/secf,efd->secd/dot_general | solution.py:49
  255.7 6.3 %copy.61 = bf16[32,4,10,2048]{3,1,2,0:T(4,128)(2,1)} copy(bf16[32,4,10,2048]{3,0,2,1:T(8,128)(2,1)S(1)} %convert_bitcast_fusion.1) | data formatting | bytes 10485760 | tf_op jit(solution)/shard_map/convert_element_type | solution.py:51
  262.0 8.0 %all-to-all-start.1 = ((bf16[32,4,10,2048]{3,1,2,0:T(4,128)(2,1)}), bf16[32,4,10,2048]{3,1,2,0:T(4,128)(2,1)}, u32[]{:S(2)}, u32[]{:S(2)}) async-start(bf16[32,4,10,2048]{3,1,2,0:T(4,128)(2,1)} %copy.61), calls=%async_computation.1 | async-start | bytes 10485760 | tf_op jit(solution)/shard_map/all_to_all | solution.py:52
  270.0 14.6 %convert_bitcast_fusion = bf16[32,4,10,2048]{3,0,2,1:T(8,128)(2,1)} fusion(bf16[4,2048,768]{2,1,0:T(8,128)(2,1)} %param.11, bf16[32,4,10,384]{3,0,2,1:T(8,128)(2,1)S(1)} %get-tuple-element.14, bf16[32,4,10,384]{3,0,2,1:T(8,128)(2,1)S(1)} %get-tuple-element.13), kind=kOutput, calls=%fused_computation.28 | convolution fusion | flops 4033085440 | bytes 19791872 | tf_op jit(solution)/shard_map/secf,edf->secd/dot_general | solution.py:67
  284.6 8.9 %copy.66 = bf16[32,4,10,2048]{3,1,2,0:T(4,128)(2,1)} copy(bf16[32,4,10,2048]{3,0,2,1:T(8,128)(2,1)} %convert_bitcast_fusion) | data formatting | bytes 10485760 | tf_op jit(solution)/shard_map/convert_element_type | solution.py:67
  293.6 51.3 %all-to-all-done.1 = bf16[32,4,10,2048]{3,1,2,0:T(4,128)(2,1)} async-done(((bf16[32,4,10,2048]{3,1,2,0:T(4,128)(2,1)}), bf16[32,4,10,2048]{3,1,2,0:T(4,128)(2,1)}, u32[]{:S(2)}, u32[]{:S(2)}) %all-to-all-start.1) | async-done | bytes 5242912 | tf_op jit(solution)/shard_map/all_to_all | solution.py:52
  344.9 10.4 %all-to-all-start.3 = ((bf16[32,4,10,2048]{3,1,2,0:T(4,128)(2,1)}), bf16[32,4,10,2048]{3,1,2,0:T(4,128)(2,1)}, u32[]{:S(2)}, u32[]{:S(2)}) async-start(bf16[32,4,10,2048]{3,1,2,0:T(4,128)(2,1)} %copy.66), calls=%async_computation.3 | async-start | bytes 10485760 | tf_op jit(solution)/shard_map/all_to_all | solution.py:70
  355.8 12.7 %copy.62 = bf16[32,4,10,2048]{3,2,1,0:T(8,128)(2,1)} copy(bf16[32,4,10,2048]{3,1,2,0:T(4,128)(2,1)} %all-to-all-done.1) | data formatting | bytes 10485760 | tf_op jit(solution)/shard_map/all_to_all | solution.py:52
  368.6 10.1 %reshape.62 = bf16[1280,2048]{1,0:T(8,128)(2,1)} reshape(bf16[32,4,10,2048]{3,2,1,0:T(8,128)(2,1)} %copy.62) | data formatting | bytes 10485760 | tf_op jit(solution)/shard_map/reshape | solution.py:54
  388.2 46.4 %all-to-all-done.3 = bf16[32,4,10,2048]{3,1,2,0:T(4,128)(2,1)} async-done(((bf16[32,4,10,2048]{3,1,2,0:T(4,128)(2,1)}), bf16[32,4,10,2048]{3,1,2,0:T(4,128)(2,1)}, u32[]{:S(2)}, u32[]{:S(2)}) %all-to-all-start.3) | async-done | bytes 5242912 | tf_op jit(solution)/shard_map/all_to_all | solution.py:70
  434.6 10.8 %copy.67 = bf16[32,4,10,2048]{3,2,1,0:T(8,128)(2,1)} copy(bf16[32,4,10,2048]{3,1,2,0:T(4,128)(2,1)} %all-to-all-done.3) | data formatting | bytes 10485760 | tf_op jit(solution)/shard_map/all_to_all | solution.py:70
  445.4 10.2 %reshape.64 = bf16[1280,2048]{1,0:T(8,128)(2,1)} reshape(bf16[32,4,10,2048]{3,2,1,0:T(8,128)(2,1)} %copy.67) | data formatting | bytes 10485760 | tf_op jit(solution)/shard_map/reshape | solution.py:70
  455.6 5.6 %gather_fusion.15 = bf16[128,2048]{1,0:T(8,128)(2,1)} fusion(bf16[1280,2048]{1,0:T(8,128)(2,1)} %reshape.64, s32[1024]{0:T(1024)S(1)} %pad_clamp_fusion), kind=kCustom, calls=%fused_computation.15.clone | custom fusion | bytes 1049088 | tf_op jit(solution)/shard_map/jit(_take)/gather | solution.py:10
  471.2 5.5 %gather_fusion.13 = bf16[128,2048]{1,0:T(8,128)(2,1)} fusion(bf16[1280,2048]{1,0:T(8,128)(2,1)} %reshape.64, s32[1024]{0:T(1024)S(1)} %pad_clamp_fusion.2), kind=kCustom, calls=%fused_computation.13.clone | custom fusion | bytes 1049088 | tf_op jit(solution)/shard_map/jit(_take)/gather | solution.py:10
  481.3 5.4 gather_fusion.12
  491.4 5.6 %gather_fusion.11 = bf16[128,2048]{1,0:T(8,128)(2,1)} fusion(bf16[1280,2048]{1,0:T(8,128)(2,1)} %reshape.64, s32[1024]{0:T(1024)S(1)} %pad_clamp_fusion.4), kind=kCustom, calls=%fused_computation.11.clone | custom fusion | bytes 1049088 | tf_op jit(solution)/shard_map/jit(_take)/gather | solution.py:10
  507.8 5.4 gather_fusion.1
  513.2 5.4 gather_fusion.9
  518.6 5.4 %gather_fusion = bf16[128,2048]{1,0:T(8,128)(2,1)} fusion(bf16[1280,2048]{1,0:T(8,128)(2,1)} %reshape.62, s32[1024]{0:T(1024)S(1)} %pad_clamp_fusion.7), kind=kCustom, calls=%fused_computation.clone | custom fusion | bytes 1049088 | tf_op jit(solution)/shard_map/jit(_take)/gather | solution.py:10
  524.0 5.4 %gather_fusion.8 = bf16[128,2048]{1,0:T(8,128)(2,1)} fusion(bf16[1280,2048]{1,0:T(8,128)(2,1)} %reshape.64, s32[1024]{0:T(1024)S(1)} %pad_clamp_fusion.7), kind=kCustom, calls=%fused_computation.8.clone | custom fusion | bytes 1049088 | tf_op jit(solution)/shard_map/jit(_take)/gather | solution.py:10
  (64 shorter events, 63.1 us)
Async XLA Ops:
  7.2 6.7 %copy-start = (bf16[128,2048]{1,0:T(8,128)(2,1)S(1)}, bf16[128,2048]{1,0:T(8,128)(2,1)}, u32[]{:S(2)}) copy-start(bf16[128,2048]{1,0:T(8,128)(2,1)} %param.9) | copy-start | bytes 1572868
  38.1 9.5 %copy-start.3 = (s32[128,8]{0,1:T(8,128)S(1)}, s32[128,8]{0,1:T(8,128)}, u32[]{:S(2)}) copy-start(s32[128,8]{0,1:T(8,128)} %param.14) | copy-start | bytes 12292
  38.1 10.3 %copy-start.2 = (bf16[128,2048]{1,0:T(8,128)(2,1)S(1)}, bf16[128,2048]{1,0:T(8,128)(2,1)}, u32[]{:S(2)}) copy-start(bf16[128,2048]{1,0:T(8,128)(2,1)} %param.10) | copy-start | bytes 1572868
  38.1 79.0 %all-to-all-start = ((bf16[32,4,10,2048]{3,1,2,0:T(4,128)(2,1)}), bf16[32,4,10,2048]{3,1,2,0:T(4,128)(2,1)}, u32[]{:S(2)}, u32[]{:S(2)}) async-start(bf16[32,4,10,2048]{3,1,2,0:T(4,128)(2,1)} %copy.59), calls=%async_computation | async-start | bytes 10485760 | tf_op jit(solution)/shard_map/all_to_all | solution.py:42
  117.1 78.3 %all-to-all-start.2 = ((bf16[32,4,10,2048]{3,1,2,0:T(4,128)(2,1)}), bf16[32,4,10,2048]{3,1,2,0:T(4,128)(2,1)}, u32[]{:S(2)}, u32[]{:S(2)}) async-start(bf16[32,4,10,2048]{3,1,2,0:T(4,128)(2,1)} %copy.64), calls=%async_computation.2 | async-start | bytes 10485760 | tf_op jit(solution)/shard_map/all_to_all | solution.py:56
  125.9 410.6 %reduce-scatter.5.cloned.1.call-start = ((), (), s32[]{:S(2)}) async-start(), calls=%async_computation.7 | async-start | bytes 7864320 | tf_op jit(solution)/shard_map/reduce_scatter | solution.py:81
  220.3 316.2 %reduce-scatter.3.cloned.1.call-start = ((), (), s32[]{:S(2)}) async-start(), calls=%async_computation.6 | async-start | bytes 15728640 | tf_op jit(solution)/shard_map/reduce_scatter | solution.py:78
  262.0 82.8 %all-to-all-start.1 = ((bf16[32,4,10,2048]{3,1,2,0:T(4,128)(2,1)}), bf16[32,4,10,2048]{3,1,2,0:T(4,128)(2,1)}, u32[]{:S(2)}, u32[]{:S(2)}) async-start(bf16[32,4,10,2048]{3,1,2,0:T(4,128)(2,1)} %copy.61), calls=%async_computation.1 | async-start | bytes 10485760 | tf_op jit(solution)/shard_map/all_to_all | solution.py:52
  344.9 89.8 %all-to-all-start.3 = ((bf16[32,4,10,2048]{3,1,2,0:T(4,128)(2,1)}), bf16[32,4,10,2048]{3,1,2,0:T(4,128)(2,1)}, u32[]{:S(2)}, u32[]{:S(2)}) async-start(bf16[32,4,10,2048]{3,1,2,0:T(4,128)(2,1)} %copy.66), calls=%async_computation.3 | async-start | bytes 10485760 | tf_op jit(solution)/shard_map/all_to_all | solution.py:70
  524.0 12.5 %copy-start.1 = (bf16[128,2048]{1,0:T(8,128)(2,1)S(1)}, bf16[128,2048]{1,0:T(8,128)(2,1)}, u32[]{:S(2)}) copy-start(bf16[128,2048]{1,0:T(8,128)(2,1)} %param.9) | copy-start | bytes 1572868
Sparse Core Ops, SparseCore 0:
  220.4 125.2 reduce-scatter.4
  349.2 140.5 reduce-scatter.2
where the time goes:
time: 554 us; the launch traced here: 544 us
  waiting for transfers between devices  195 us (35%)
  local copies, waits for them, and re-layouts  185 us (33%)
  matrix products  98.3 us (18%)
  starting transfers between devices  37.4 us (7%)
  between operations  14.8 us (3%)
  other arithmetic  13.1 us (2%)
    gather x16, local copies, waits for them, and re-layouts, gather_routes(): picked = jnp.take(rows, position[:, k], axis=0).astype(jnp.float32)  83.4 us
    all_to_all x1, waiting for transfers between devices, body(): lax.all_to_all((to_slots(d_mixed) * slot_gate[:, None]).astype(jnp.bfloat...  53.3 us
    all_to_all x1, waiting for transfers between devices, body(): lax.all_to_all(expert_out, 'expert', split_axis=0, concat_axis=0, tiled=T...  51.3 us
    all_to_all x1, waiting for transfers between devices, body(): lax.all_to_all(d_rows, 'expert', split_axis=0, concat_axis=0, tiled=True)  46.4 us
    all_to_all x1, waiting for transfers between devices, body(): lax.all_to_all(x_send, 'expert', split_axis=0, concat_axis=0, tiled=True)  44.4 us
    dot_general x1, matrix products, body(): jnp.einsum('secd,secf->edf', x_recv, d_pre, preferred_element_type=jnp.fl...  28.8 us
    reshape x2, local copies, waits for them, and re-layouts, body(): (to_slots(d_mixed) * slot_gate[:, None]).astype(jnp.bfloat16)  20.3 us
    reshape x2, local copies, waits for them, and re-layouts, body(): x_send = to_slots(tokens).astype(jnp.bfloat16).reshape(blocked)  20.2 us
  transfers between devices with their start and end apart: 6, of which 4 were waited for; matrix products, arithmetic and copies ran while one was open for 44% of the time, Pallas kernels for 0%

commit v1 on v0

v1 whole, which is shorter than its diff:
```python
import jax
import jax.numpy as jnp
from jax import lax
from jax.sharding import PartitionSpec as P

CAP = 10
F32 = jnp.float32
BF16 = jnp.bfloat16
ALL = ("dp", "expert")


def body(tokens, d_mixed, w_in, w_out, expert_ids, gate_fixed, placement):
    tok_rows, width = tokens.shape
    copies = lax.axis_size("dp")
    holders = lax.axis_size("expert")
    hidden = w_out.shape[1]
    devices = copies * holders
    main, rest = 8, CAP - 8
    gates = gate_fixed.astype(F32)
    gates = gates / jnp.sum(gates, axis=1, keepdims=True)
    catalog = jnp.arange(devices, dtype=jnp.int32)
    home = (placement % copies) * holders + placement // copies
    target = jnp.sum(jnp.where(expert_ids[:, :, None] == catalog, home, 0), axis=2)
    hits = target[:, :, None] == catalog
    sent = jnp.any(hits, axis=1)
    weight = jnp.sum(jnp.where(hits, gates[:, :, None], 0.0), axis=1)
    t_ids = jnp.arange(tok_rows, dtype=jnp.int32)
    before = (t_ids[:, None] > t_ids[None, :]).astype(BF16)
    rank = jnp.dot(before, sent.astype(BF16), preferred_element_type=F32).astype(jnp.int32)
    rank = jnp.where(sent, rank, -1).T
    weight = weight.T

    def picks(first, count):
        ranks = first + jnp.arange(count, dtype=jnp.int32)
        pick = rank[:, None, :] == ranks[None, :, None]
        gate = jnp.where(pick, weight[:, None, :], 0.0)
        high = gate.astype(BF16)
        low = (gate - high.astype(F32)).astype(BF16)
        flat = (devices * count, tok_rows)
        return (
            pick.astype(BF16).reshape(flat),
            jnp.sum(gate, axis=2).reshape(-1, 1),
            high.reshape(flat),
            low.reshape(flat),
        )

    parts = [picks(0, main), picks(main, rest)]
    counts = [main, rest]

    def exchange(rows, count):
        return lax.all_to_all(
            rows.reshape(devices, count, width), ALL, split_axis=0, concat_axis=0, tiled=True
        ).reshape(devices * count, width)

    def dispatch(rows, gated):
        out = []
        for (pick, scale, _, _), count in zip(parts, counts):
            chosen = jnp.dot(pick, rows, preferred_element_type=F32)
            if gated:
                chosen = chosen * scale
            out.append(exchange(chosen.astype(BF16), count))
        return jnp.concatenate(out, axis=0)

    def send_back(rows):
        cut = devices * main
        return [exchange(rows[:cut], main), exchange(rows[cut:], rest)]

    mine = lax.axis_index("dp")
    wi = lax.dynamic_index_in_dim(w_in, mine, 0, keepdims=False)
    wo = lax.dynamic_index_in_dim(w_out, mine, 0, keepdims=False)
    x = dispatch(tokens, False)
    d = dispatch(d_mixed, True)
    pre = jnp.dot(x, wi, preferred_element_type=F32)
    gate, up = pre[:, :hidden], pre[:, hidden:]
    sig = jax.nn.sigmoid(gate)
    silu = gate * sig
    act = (silu * up).astype(BF16)
    out = jnp.dot(act, wo, preferred_element_type=F32).astype(BF16)
    back = send_back(out)
    d_act = lax.dot_general(d, wo, (((1,), (1,)), ((), ())), preferred_element_type=F32)
    d_pre = jnp.concatenate(
        [d_act * up * sig * (1.0 + gate * (1.0 - sig)), d_act * silu], axis=1
    ).astype(BF16)
    d_rows = lax.dot_general(d_pre, wi, (((1,), (1,)), ((), ())), preferred_element_type=F32)
    returned = send_back(d_rows.astype(BF16))
    over_rows = (((0,), (0,)), ((), ()))
    g_in = lax.dot_general(x, d_pre, over_rows, preferred_element_type=F32).astype(BF16)
    g_out = lax.dot_general(act, d, over_rows, preferred_element_type=F32).astype(BF16)
    share = width // copies
    grad_in = lax.all_to_all(
        g_in.reshape(copies, share, 2 * hidden), "dp", split_axis=0, concat_axis=0, tiled=True
    )
    grad_out = lax.all_to_all(
        jnp.transpose(g_out.reshape(hidden, copies, share), (1, 0, 2)),
        "dp",
        split_axis=0,
        concat_axis=0,
        tiled=True,
    )
    mixed = jnp.zeros((tok_rows, width), F32)
    d_tokens = jnp.zeros((tok_rows, width), F32)
    for (pick, _, high, low), rows, d_part in zip(parts, back, returned):
        for table in (high, low):
            mixed = mixed + lax.dot_general(table, rows, over_rows, preferred_element_type=F32)
        d_tokens = d_tokens + lax.dot_general(pick, d_part, over_rows, preferred_element_type=F32)
    return mixed.astype(BF16), d_tokens.astype(BF16), grad_in, grad_out


def solution(mesh):
    in_specs = (
        P(ALL, None),
        P(ALL, None),
        P("expert", None, None),
        P("expert", None, None),
        P(ALL, None),
        P(ALL, None),
        P(),
    )
    out_specs = (P(ALL, None), P(ALL, None), P("expert", "dp", None), P("expert", None, "dp"))
    return jax.shard_map(body, mesh=mesh, in_specs=in_specs, out_specs=out_specs, check_vma=False)
```

time: 554 us -> 454 us (0.82)
  local copies, waits for them, and re-layouts: 185 us -> 30.9 us
  waiting for transfers between devices: 195 us -> 279 us
  matrix products: 98.3 us -> 69 us
  starting transfers between devices: 37.4 us -> 59.2 us
  between operations: 14.8 us -> 1.23 us
  other arithmetic: 13.1 us -> 5.94 us
    all_to_all x4 -> x10, waiting for transfers between devices: 195 us -> 279 us  [the longest x8 233 us: exchange(): lax.all_to_all(rows.reshape(devices, count, width), ALL, split_axis=0, co...]
    gather x16 -> x0, local copies, waits for them, and re-layouts: 83.4 us -> none  [gather_routes(): picked = jnp.take(rows, position[:, k], axis=0).astype(jnp.float32)]
    reshape x6 -> x9, local copies, waits for them, and re-layouts: 60.8 us -> 18.5 us  [the longest x6 15.6 us: exchange(): rows.reshape(devices, count, width)]
    dot_general x8 -> x17, matrix products: 98.3 us -> 69 us  [the longest x4 11.2 us: body(): lax.dot_general(table, rows, over_rows, preferred_element_type=F32)]
    all_to_all x2 -> x0, local copies, waits for them, and re-layouts: 23.6 us -> none  [the longest x1 12.7 us: body(): lax.all_to_all(expert_out, 'expert', split_axis=0, concat_axis=0, tiled=T...]
    all_to_all x4 -> x10, starting transfers between devices: 36.7 us -> 59.2 us  [the longest x8 51 us: exchange(): lax.all_to_all(rows.reshape(devices, count, width), ALL, split_axis=0, co...]
    convert_element_type x2 -> x0, local copies, waits for them, and re-layouts: 15.2 us -> none  [the longest x1 8.91 us: body(): jnp.einsum('secf,edf->secd', d_pre, w_in, preferred_element_type=jnp.floa...]
    unnamed x9 -> x33, local copies, waits for them, and re-layouts: 0.87 us -> 11.4 us
  transfers between devices with their start and end apart: 6 -> 10, of which waited for: 4 -> 10; matrix products, arithmetic and copies ran while one was open for 44% -> 14% of each run, Pallas kernels for 0% -> 0%
where the time goes in v1:
time: 454 us; the launch traced here: 446 us
  waiting for transfers between devices  279 us (61%)
  matrix products  69 us (15%)
  starting transfers between devices  59.2 us (13%)
  local copies, waits for them, and re-layouts  30.9 us (7%)
  other arithmetic  5.94 us (1%)
    all_to_all x8, waiting for transfers between devices, exchange(): lax.all_to_all(rows.reshape(devices, count, width), ALL, split_axis=0, co...  233 us
    all_to_all x8, starting transfers between devices, exchange(): lax.all_to_all(rows.reshape(devices, count, width), ALL, split_axis=0, co...  51 us
    all_to_all x1, waiting for transfers between devices, body(): lax.all_to_all(g_in.reshape(copies, share, 2 * hidden), 'dp', split_axis=...  33.8 us
    reshape x6, local copies, waits for them, and re-layouts, exchange(): rows.reshape(devices, count, width)  15.6 us
    all_to_all x1, waiting for transfers between devices, body(): lax.all_to_all(jnp.transpose(g_out.reshape(hidden, copies, share), (1, 0,...  12.5 us
    unnamed x33, local copies, waits for them, and re-layouts  11.4 us
    dot_general x4, matrix products, body(): lax.dot_general(table, rows, over_rows, preferred_element_type=F32)  11.2 us
    dot_general x1, matrix products, body(): pre = jnp.dot(x, wi, preferred_element_type=F32)  9.74 us
  transfers between devices with their start and end apart: 10, of which 10 were waited for; matrix products, arithmetic and copies ran while one was open for 14% of the time, Pallas kernels for 0%

profile of v1, /device:TPU:0, one launch (start us, length us, event | category | flops | bytes accessed | tf_op | source)
XLA Modules:
  0.0 445.5 jit_solution(8107897557302455301)
XLA Ops:
  10.8 11.1 %all-to-all-start.5 = ((bf16[128,2,2048]{2,1,0:T(2,128)(2,1)}), bf16[128,2,2048]{2,1,0:T(2,128)(2,1)S(1)}, u32[]{:S(2)}, u32[]{:S(2)}) async-start(bf16[128,2,2048]{2,1,0:T(2,128)(2,1)} %reshape.86), calls=%async_computation.5 | async-start | bytes 2097152 | tf_op jit(solution)/shard_map/all_to_all | solution.py:51
  23.9 17.1 %all-to-all-done.5 = bf16[128,2,2048]{2,1,0:T(2,128)(2,1)S(1)} async-done(((bf16[128,2,2048]{2,1,0:T(2,128)(2,1)}), bf16[128,2,2048]{2,1,0:T(2,128)(2,1)S(1)}, u32[]{:S(2)}, u32[]{:S(2)}) %all-to-all-start.5) | async-done | bytes 1048608 | tf_op jit(solution)/shard_map/all_to_all | solution.py:51
  41.0 4.6 %all-to-all-start.1 = ((bf16[128,2,2048]{2,1,0:T(2,128)(2,1)}), bf16[128,2,2048]{2,1,0:T(2,128)(2,1)S(1)}, u32[]{:S(2)}, u32[]{:S(2)}) async-start(bf16[128,2,2048]{2,1,0:T(2,128)(2,1)} %reshape.80), calls=%async_computation.1 | async-start | bytes 2097152 | tf_op jit(solution)/shard_map/all_to_all | solution.py:51
  49.0 15.7 %all-to-all-done.1 = bf16[128,2,2048]{2,1,0:T(2,128)(2,1)S(1)} async-done(((bf16[128,2,2048]{2,1,0:T(2,128)(2,1)}), bf16[128,2,2048]{2,1,0:T(2,128)(2,1)S(1)}, u32[]{:S(2)}, u32[]{:S(2)}) %all-to-all-start.1) | async-done | bytes 1048608 | tf_op jit(solution)/shard_map/all_to_all | solution.py:51
  64.7 5.8 %all-to-all-start = ((bf16[128,8,2048]{2,1,0:T(8,128)(2,1)}), bf16[128,8,2048]{2,1,0:T(8,128)(2,1)}, u32[]{:S(2)}, u32[]{:S(2)}) async-start(bf16[128,8,2048]{2,1,0:T(8,128)(2,1)} %convert_bitcast_fusion), calls=%async_computation | async-start | bytes 8388608 | tf_op jit(solution)/shard_map/all_to_all | solution.py:51
  74.1 48.0 %all-to-all-done = bf16[128,8,2048]{2,1,0:T(8,128)(2,1)} async-done(((bf16[128,8,2048]{2,1,0:T(8,128)(2,1)}), bf16[128,8,2048]{2,1,0:T(8,128)(2,1)}, u32[]{:S(2)}, u32[]{:S(2)}) %all-to-all-start) | async-done | bytes 4194336 | tf_op jit(solution)/shard_map/all_to_all | solution.py:51
  122.1 6.7 %all-to-all-start.4 = ((bf16[128,8,2048]{2,1,0:T(8,128)(2,1)}), bf16[128,8,2048]{2,1,0:T(8,128)(2,1)}, u32[]{:S(2)}, u32[]{:S(2)}) async-start(bf16[128,8,2048]{2,1,0:T(8,128)(2,1)} %fusion.3), calls=%async_computation.4 | async-start | bytes 8388608 | tf_op jit(solution)/shard_map/all_to_all | solution.py:51
  130.5 9.7 %fusion.2 = f32[1280,768]{0,1:T(8,128)} fusion(bf16[256,2048]{1,0:T(8,128)(2,1)S(1)} %reshape.81, bf16[1024,2048]{1,0:T(8,128)(2,1)} %bitcast.4, bf16[4,2048,768]{2,1,0:T(8,128)(2,1)} %param.9, s32[]{:T(128)S(6)} %select_n.45), kind=kOutput, calls=%fused_computation.11 | convolution fusion | flops 4037017600 | bytes 12320772 | tf_op jit(solution)/shard_map/dot_general | solution.py:73
  140.2 40.2 %all-to-all-done.4 = bf16[128,8,2048]{2,1,0:T(8,128)(2,1)} async-done(((bf16[128,8,2048]{2,1,0:T(8,128)(2,1)}), bf16[128,8,2048]{2,1,0:T(8,128)(2,1)}, u32[]{:S(2)}, u32[]{:S(2)}) %all-to-all-start.4) | async-done | bytes 4194336 | tf_op jit(solution)/shard_map/all_to_all | solution.py:51
  180.4 7.7 %multiply_convert_fusion.2 = (bf16[1280,384]{0,1:T(8,128)(2,1)S(1)}, bf16[1280,384]{0,1:T(8,128)(2,1)S(1)}, bf16[1280,384]{0,1:T(8,128)(2,1)}) fusion(f32[1280,768]{0,1:T(8,128)} %fusion.2, bf16[4,384,2048]{2,1,0:T(8,128)(2,1)} %param.10, s32[]{:T(128)S(6)} %select_n.45, bf16[256,2048]{1,0:T(8,128)(2,1)S(1)} %copy-done.10, bf16[1024,2048]{1,0:T(8,128)(2,1)} %bitcast.14), kind=kOutput, calls=%fused_computation.35 | convolution fusion | flops 2031124480 | bytes 13697028 | tf_op jit(solution)/shard_map/dot_general | solution.py:80
  188.1 7.2 %convolution_convert_fusion = bf16[1280,2048]{1,0:T(8,128)(2,1)S(1)} fusion(bf16[4,2048,768]{2,1,0:T(8,128)(2,1)} %param.9, s32[]{:T(128)S(6)} %select_n.45, bf16[1280,384]{0,1:T(8,128)(2,1)S(1)} %get-tuple-element.7, bf16[1280,384]{0,1:T(8,128)(2,1)S(1)} %get-tuple-element.6), kind=kOutput, calls=%fused_computation.1 | convolution fusion | flops 4033085440 | bytes 10354692 | tf_op jit(solution)/shard_map/dot_general | solution.py:84
  199.1 5.7 %all-to-all-start.7 = ((bf16[128,2,2048]{2,1,0:T(2,128)(2,1)}), bf16[128,2,2048]{2,1,0:T(2,128)(2,1)S(1)}, u32[]{:S(2)}, u32[]{:S(2)}) async-start(bf16[128,2,2048]{2,1,0:T(2,128)(2,1)} %reshape.89), calls=%async_computation.7 | async-start | bytes 2097152 | tf_op jit(solution)/shard_map/all_to_all | solution.py:51
  204.9 4.6 %convolution_convert_fusion.1 = bf16[1280,2048]{1,0:T(8,128)(2,1)S(1)} fusion(bf16[1280,384]{0,1:T(8,128)(2,1)S(1)} %copy-done.12, bf16[4,384,2048]{2,1,0:T(8,128)(2,1)} %param.10, s32[]{:T(128)S(6)} %select_n.45), kind=kOutput, calls=%fused_computation.2 | convolution fusion | flops 2015887360 | bytes 7798788 | tf_op jit(solution)/shard_map/dot_general | solution.py:78
  213.4 10.5 %all-to-all-done.7 = bf16[128,2,2048]{2,1,0:T(2,128)(2,1)S(1)} async-done(((bf16[128,2,2048]{2,1,0:T(2,128)(2,1)}), bf16[128,2,2048]{2,1,0:T(2,128)(2,1)S(1)}, u32[]{:S(2)}, u32[]{:S(2)}) %all-to-all-start.7) | async-done | bytes 1048608 | tf_op jit(solution)/shard_map/all_to_all | solution.py:51
  224.9 4.6 %all-to-all-start.3 = ((bf16[128,2,2048]{2,1,0:T(2,128)(2,1)}), bf16[128,2,2048]{2,1,0:T(2,128)(2,1)S(1)}, u32[]{:S(2)}, u32[]{:S(2)}) async-start(bf16[128,2,2048]{2,1,0:T(2,128)(2,1)} %reshape.83), calls=%async_computation.3 | async-start | bytes 2097152 | tf_op jit(solution)/shard_map/all_to_all | solution.py:51
  229.5 5.0 %fusion.6 = bf16[384,2048]{1,0:T(8,128)(2,1)S(1)} fusion(bf16[1280,384]{0,1:T(8,128)(2,1)} %get-tuple-element.8, bf16[256,2048]{1,0:T(8,128)(2,1)} %reshape.87, bf16[1024,2048]{1,0:T(8,128)(2,1)} %bitcast.14), kind=kOutput, calls=%fused_computation.15 | convolution fusion | flops 2024538112 | bytes 7798784 | tf_op jit(solution)/shard_map/dot_general | solution.py:88
  235.8 12.7 %all-to-all-done.3 = bf16[128,2,2048]{2,1,0:T(2,128)(2,1)S(1)} async-done(((bf16[128,2,2048]{2,1,0:T(2,128)(2,1)}), bf16[128,2,2048]{2,1,0:T(2,128)(2,1)S(1)}, u32[]{:S(2)}, u32[]{:S(2)}) %all-to-all-start.3) | async-done | bytes 1048608 | tf_op jit(solution)/shard_map/all_to_all | solution.py:51
  248.6 3.6 all-to-all-start.9
  252.2 9.1 %convolution_convert_fusion.2 = bf16[2048,768]{1,0:T(8,128)(2,1)} fusion(bf16[256,2048]{1,0:T(8,128)(2,1)} %copy-done.9, bf16[1024,2048]{1,0:T(8,128)(2,1)} %bitcast.4, bf16[1280,384]{0,1:T(8,128)(2,1)} %copy-done.14, bf16[1280,384]{0,1:T(8,128)(2,1)} %copy-done.13), kind=kOutput, calls=%fused_computation.8 | convolution fusion | flops 4042522624 | bytes 10354688 | tf_op jit(solution)/shard_map/dot_general | solution.py:87
  261.2 12.5 %all-to-all-done.9 = bf16[4,384,512]{2,1,0:T(8,128)(2,1)S(1)} async-done(((bf16[4,384,512]{2,1,0:T(8,128)(2,1)}), bf16[4,384,512]{2,1,0:T(8,128)(2,1)S(1)}, u32[]{:S(2)}, u32[]{:S(2)}) %all-to-all-start.9) | async-done | bytes 1572896 | tf_op jit(solution)/shard_map/all_to_all | solution.py:93
  273.7 4.7 %all-to-all-start.8 = ((bf16[4,512,768]{2,1,0:T(8,128)(2,1)}), bf16[4,512,768]{2,1,0:T(8,128)(2,1)}, u32[]{:S(2)}, u32[]{:S(2)}) async-start(bf16[4,512,768]{2,1,0:T(8,128)(2,1)} %bitcast.74), calls=%async_computation.8 | async-start | bytes 6291456 | tf_op jit(solution)/shard_map/all_to_all | solution.py:90
  278.4 4.7 %slice_bitcast_fusion.1 = bf16[128,8,2048]{2,1,0:T(8,128)(2,1)} fusion(bf16[1280,2048]{1,0:T(8,128)(2,1)} %copy-done.3), kind=kLoop, calls=%fused_computation.6 | loop fusion | bytes 8388608 | tf_op jit(solution)/shard_map/reshape | solution.py:52
  283.1 33.8 %all-to-all-done.8 = bf16[4,512,768]{2,1,0:T(8,128)(2,1)} async-done(((bf16[4,512,768]{2,1,0:T(8,128)(2,1)}), bf16[4,512,768]{2,1,0:T(8,128)(2,1)}, u32[]{:S(2)}, u32[]{:S(2)}) %all-to-all-start.8) | async-done | bytes 3145760 | tf_op jit(solution)/shard_map/all_to_all | solution.py:90
  316.9 5.8 %all-to-all-start.2 = ((bf16[128,8,2048]{2,1,0:T(8,128)(2,1)}), bf16[128,8,2048]{2,1,0:T(8,128)(2,1)}, u32[]{:S(2)}, u32[]{:S(2)}) async-start(bf16[128,8,2048]{2,1,0:T(8,128)(2,1)} %slice_bitcast_fusion.1), calls=%async_computation.2 | async-start | bytes 8388608 | tf_op jit(solution)/shard_map/all_to_all | solution.py:51
  322.7 4.9 %slice_bitcast_fusion = bf16[128,8,2048]{2,1,0:T(8,128)(2,1)} fusion(bf16[1280,2048]{1,0:T(8,128)(2,1)} %copy-done.2), kind=kLoop, calls=%fused_computation.5 | loop fusion | bytes 8388608 | tf_op jit(solution)/shard_map/reshape | solution.py:52
  327.6 46.7 %all-to-all-done.2 = bf16[128,8,2048]{2,1,0:T(8,128)(2,1)} async-done(((bf16[128,8,2048]{2,1,0:T(8,128)(2,1)}), bf16[128,8,2048]{2,1,0:T(8,128)(2,1)}, u32[]{:S(2)}, u32[]{:S(2)}) %all-to-all-start.2) | async-done | bytes 4194336 | tf_op jit(solution)/shard_map/all_to_all | solution.py:51
  374.3 6.5 %all-to-all-start.6 = ((bf16[128,8,2048]{2,1,0:T(8,128)(2,1)}), bf16[128,8,2048]{2,1,0:T(8,128)(2,1)}, u32[]{:S(2)}, u32[]{:S(2)}) async-start(bf16[128,8,2048]{2,1,0:T(8,128)(2,1)} %slice_bitcast_fusion), calls=%async_computation.6 | async-start | bytes 8388608 | tf_op jit(solution)/shard_map/all_to_all | solution.py:51
  386.2 3.9 convolution_bitcast_fusion.4
  390.1 42.2 %all-to-all-done.6 = bf16[128,8,2048]{2,1,0:T(8,128)(2,1)} async-done(((bf16[128,8,2048]{2,1,0:T(8,128)(2,1)}), bf16[128,8,2048]{2,1,0:T(8,128)(2,1)}, u32[]{:S(2)}, u32[]{:S(2)}) %all-to-all-start.6) | async-done | bytes 4194336 | tf_op jit(solution)/shard_map/all_to_all | solution.py:51
  432.3 4.2 fusion.15
  436.6 3.8 fusion.14
  440.4 3.8 copy.77
  (71 shorter events, 37.2 us)
Async XLA Ops:
  0.6 21.3 %copy-start = (bf16[128,2048]{1,0:T(8,128)(2,1)S(1)}, bf16[128,2048]{1,0:T(8,128)(2,1)}, u32[]{:S(2)}) copy-start(bf16[128,2048]{1,0:T(8,128)(2,1)} %param.7) | copy-start | bytes 1572868
  10.8 30.2 %all-to-all-start.5 = ((bf16[128,2,2048]{2,1,0:T(2,128)(2,1)}), bf16[128,2,2048]{2,1,0:T(2,128)(2,1)S(1)}, u32[]{:S(2)}, u32[]{:S(2)}) async-start(bf16[128,2,2048]{2,1,0:T(2,128)(2,1)} %reshape.86), calls=%async_computation.5 | async-start | bytes 2097152 | tf_op jit(solution)/shard_map/all_to_all | solution.py:51
  41.0 23.7 %all-to-all-start.1 = ((bf16[128,2,2048]{2,1,0:T(2,128)(2,1)}), bf16[128,2,2048]{2,1,0:T(2,128)(2,1)S(1)}, u32[]{:S(2)}, u32[]{:S(2)}) async-start(bf16[128,2,2048]{2,1,0:T(2,128)(2,1)} %reshape.80), calls=%async_computation.1 | async-start | bytes 2097152 | tf_op jit(solution)/shard_map/all_to_all | solution.py:51
  49.0 21.8 %copy-start.11 = (bf16[128,2048]{1,0:T(8,128)(2,1)S(1)}, bf16[128,2048]{1,0:T(8,128)(2,1)}, u32[]{:S(2)}) copy-start(bf16[128,2048]{1,0:T(8,128)(2,1)} %param.8) | copy-start | bytes 1572868
  64.7 57.4 %all-to-all-start = ((bf16[128,8,2048]{2,1,0:T(8,128)(2,1)}), bf16[128,8,2048]{2,1,0:T(8,128)(2,1)}, u32[]{:S(2)}, u32[]{:S(2)}) async-start(bf16[128,8,2048]{2,1,0:T(8,128)(2,1)} %convert_bitcast_fusion), calls=%async_computation | async-start | bytes 8388608 | tf_op jit(solution)/shard_map/all_to_all | solution.py:51
  122.1 58.3 %all-to-all-start.4 = ((bf16[128,8,2048]{2,1,0:T(8,128)(2,1)}), bf16[128,8,2048]{2,1,0:T(8,128)(2,1)}, u32[]{:S(2)}, u32[]{:S(2)}) async-start(bf16[128,8,2048]{2,1,0:T(8,128)(2,1)} %fusion.3), calls=%async_computation.4 | async-start | bytes 8388608 | tf_op jit(solution)/shard_map/all_to_all | solution.py:51
  130.5 9.8 %copy-start.9 = (bf16[256,2048]{1,0:T(8,128)(2,1)}, bf16[256,2048]{1,0:T(8,128)(2,1)S(1)}, u32[]{:S(2)}) copy-start(bf16[256,2048]{1,0:T(8,128)(2,1)S(1)} %reshape.81) | copy-start | bytes 3145732
  130.5 49.9 %copy-start.10 = (bf16[256,2048]{1,0:T(8,128)(2,1)S(1)}, bf16[256,2048]{1,0:T(8,128)(2,1)}, u32[]{:S(2)}) copy-start(bf16[256,2048]{1,0:T(8,128)(2,1)} %reshape.87) | copy-start | bytes 3145732
  188.1 7.2 %copy-start.13 = (bf16[1280,384]{0,1:T(8,128)(2,1)}, bf16[1280,384]{0,1:T(8,128)(2,1)S(1)}, u32[]{:S(2)}) copy-start(bf16[1280,384]{0,1:T(8,128)(2,1)S(1)} %get-tuple-element.6) | copy-start | bytes 2949124
  188.1 7.2 %copy-start.14 = (bf16[1280,384]{0,1:T(8,128)(2,1)}, bf16[1280,384]{0,1:T(8,128)(2,1)S(1)}, u32[]{:S(2)}) copy-start(bf16[1280,384]{0,1:T(8,128)(2,1)S(1)} %get-tuple-element.7) | copy-start | bytes 2949124
  195.3 2.3 copy-start.2
  197.6 7.3 %copy-start.12 = (bf16[1280,384]{0,1:T(8,128)(2,1)S(1)}, bf16[1280,384]{0,1:T(8,128)(2,1)}, u32[]{:S(2)}) copy-start(bf16[1280,384]{0,1:T(8,128)(2,1)} %get-tuple-element.8) | copy-start | bytes 2949124
  199.1 24.8 %all-to-all-start.7 = ((bf16[128,2,2048]{2,1,0:T(2,128)(2,1)}), bf16[128,2,2048]{2,1,0:T(2,128)(2,1)S(1)}, u32[]{:S(2)}, u32[]{:S(2)}) async-start(bf16[128,2,2048]{2,1,0:T(2,128)(2,1)} %reshape.89), calls=%async_computation.7 | async-start | bytes 2097152 | tf_op jit(solution)/shard_map/all_to_all | solution.py:51
  209.5 2.4 copy-start.3
  223.9 1.0 copy-start.6
  224.9 23.7 %all-to-all-start.3 = ((bf16[128,2,2048]{2,1,0:T(2,128)(2,1)}), bf16[128,2,2048]{2,1,0:T(2,128)(2,1)S(1)}, u32[]{:S(2)}, u32[]{:S(2)}) async-start(bf16[128,2,2048]{2,1,0:T(2,128)(2,1)} %reshape.83), calls=%async_computation.3 | async-start | bytes 2097152 | tf_op jit(solution)/shard_map/all_to_all | solution.py:51
  248.6 25.1 %all-to-all-start.9 = ((bf16[4,384,512]{2,1,0:T(8,128)(2,1)}), bf16[4,384,512]{2,1,0:T(8,128)(2,1)S(1)}, u32[]{:S(2)}, u32[]{:S(2)}) async-start(bf16[4,384,512]{2,1,0:T(8,128)(2,1)} %bitcast.73), calls=%async_computation.9 | async-start | bytes 3145728 | tf_op jit(solution)/shard_map/all_to_all | solution.py:93
  273.7 43.2 %all-to-all-start.8 = ((bf16[4,512,768]{2,1,0:T(8,128)(2,1)}), bf16[4,512,768]{2,1,0:T(8,128)(2,1)}, u32[]{:S(2)}, u32[]{:S(2)}) async-start(bf16[4,512,768]{2,1,0:T(8,128)(2,1)} %bitcast.74), calls=%async_computation.8 | async-start | bytes 6291456 | tf_op jit(solution)/shard_map/all_to_all | solution.py:90
  316.9 57.4 %all-to-all-start.2 = ((bf16[128,8,2048]{2,1,0:T(8,128)(2,1)}), bf16[128,8,2048]{2,1,0:T(8,128)(2,1)}, u32[]{:S(2)}, u32[]{:S(2)}) async-start(bf16[128,8,2048]{2,1,0:T(8,128)(2,1)} %slice_bitcast_fusion.1), calls=%async_computation.2 | async-start | bytes 8388608 | tf_op jit(solution)/shard_map/all_to_all | solution.py:51
  374.3 58.1 %all-to-all-start.6 = ((bf16[128,8,2048]{2,1,0:T(8,128)(2,1)}), bf16[128,8,2048]{2,1,0:T(8,128)(2,1)}, u32[]{:S(2)}, u32[]{:S(2)}) async-start(bf16[128,8,2048]{2,1,0:T(8,128)(2,1)} %slice_bitcast_fusion), calls=%async_computation.6 | async-start | bytes 8388608 | tf_op jit(solution)/shard_map/all_to_all | solution.py:51
  380.8 3.7 copy-start.7
  390.1 46.4 %copy-start.4 = (f32[128,2048]{1,0:T(8,128)S(1)}, f32[128,2048]{1,0:T(8,128)}, u32[]{:S(2)}) copy-start(f32[128,2048]{1,0:T(8,128)} %convolution_bitcast_fusion.2) | copy-start | bytes 3145732
  432.3 4.2 copy-start.5
  432.3 4.2 copy-start.8
  436.6 8.7 %copy-start.1 = (bf16[128,2048]{1,0:T(8,128)(2,1)S(1)}, bf16[128,2048]{1,0:T(8,128)(2,1)}, u32[]{:S(2)}) copy-start(bf16[128,2048]{1,0:T(8,128)(2,1)} %param.7) | copy-start | bytes 1572868

commit v2 on v1

v2 whole, which is shorter than its diff:
```python
import jax
import jax.numpy as jnp
from jax import lax
from jax.experimental import pallas as pl
from jax.experimental.pallas import tpu as pltpu
from jax.sharding import PartitionSpec as P

CAP = 10
F32 = jnp.float32
BF16 = jnp.bfloat16
ALL = ("dp", "expert")
MESH = pl.DeviceIdType.MESH
RING, PLANE, CORES = 4, 16, 2
PEERS = PLANE * CORES
CHUNKS, GROUPS, TILE = 4, 5, 8
ROWS = PEERS * TILE


def dot(a, b, dims):
    return lax.dot_general(a, b, (dims, ((), ())), preferred_element_type=F32)


def flat(block):
    return block.reshape(ROWS, block.shape[-1])


def kernel(
    tokens, d_mixed, tables, w_in, w_out,
    mixed, d_tokens, grad_in, grad_out,
    x_own, d_own, x_send, d_send, x_recv, d_recv, o_recv, r_recv, m_recv, t_recv,
    tabs, wi, wo, pick, scale, back, gated, pre, act, d_pre, g_in, g_out,
    w_sem, tab_s, tab_r, own_s, own_r, send, recv, part_s, part_r, gi_s, gi_r, go_s, go_r,
):
    dp, ex = lax.axis_index("dp"), lax.axis_index("expert")
    y = (dp // CORES) * 2 + ex // PLANE
    core, place = dp % CORES, ex % PLANE
    me = core * PLANE + place
    wide = x_send.shape[-1]
    hidden = act.shape[-1]

    def ring_id(other):
        return ((other // 2) * CORES + core, (other % 2) * PLANE + place)

    def plane_id(other):
        return ((dp // CORES) * CORES + other // PLANE, (ex // PLANE) * PLANE + other % PLANE)

    def remote(src, dst, s, r, device):
        return pltpu.make_async_remote_copy(
            src_ref=src, dst_ref=dst, send_sem=s, recv_sem=r, device_id=device, device_id_type=MESH
        )

    def await_bytes(ref, sem):
        pltpu.make_async_copy(ref, ref, sem).wait()

    get_wi = pltpu.make_async_copy(w_in.at[dp], wi, w_sem.at[0])
    get_wo = pltpu.make_async_copy(w_out.at[dp], wo, w_sem.at[1])

    for i in range(1, RING):
        other = (y + i) % RING
        remote(tables.at[other], tabs.at[y], tab_s, tab_r, ring_id(other)).start()
    pltpu.make_async_copy(tables.at[y], tabs.at[y], tab_r).start()

    def spread(n, rows, own):
        for c in range(CHUNKS):
            part = rows.at[:, pl.ds(c * wide, wide)]
            for i in range(1, RING):
                other = (y + i) % RING
                remote(part, own.at[c, y], own_s.at[n, c], own_r.at[n, c], ring_id(other)).start()
            pltpu.make_async_copy(part, own.at[c, y], own_r.at[n, c]).start()

    spread(0, tokens, x_own)
    get_wi.start()
    get_wo.start()
    spread(1, d_mixed, d_own)

    await_bytes(tabs, tab_r)
    code = jnp.concatenate([tabs[s, 0] for s in range(RING)], axis=1)
    gate = jnp.concatenate([tabs[s, 1] for s in range(RING)], axis=1)
    row = lax.broadcasted_iota(jnp.int32, (PEERS, TILE, code.shape[1]), 1).astype(F32)

    for a in range(GROUPS):
        hit = code[:, None, :] == row + F32(a * TILE)
        ones = jnp.where(hit, 1.0, 0.0).astype(F32)
        pick[a] = flat(ones).astype(BF16)
        scale[a] = flat(jnp.sum(ones * gate[:, None, :], axis=2, keepdims=True))

    def exchange(n, c, out, into):
        def one(i, carry):
            other = (me + i) % PEERS
            remote(
                out.at[c, :, other], into.at[c, :, me], send.at[n, c], recv.at[n, c], plane_id(other)
            ).start()
            return carry

        lax.fori_loop(1, PEERS, one, 0)
        pltpu.make_async_copy(out.at[c, :, me], into.at[c, :, me], recv.at[n, c]).start()

    def sent(n, c, out):
        await_bytes(out.at[c, :, pl.ds(0, PEERS - 1)], send.at[n, c])

    def put(out, c, a, rows):
        out[c, a] = rows.reshape(PEERS, TILE, rows.shape[-1]).astype(BF16)

    def choose(n, own, out, into, gated_by):
        def chunk(c, carry):
            await_bytes(own.at[c], own_r.at[n, c])
            source = own[c].reshape(-1, wide)

            def group(a, carry):
                rows = dot(pick[a], source, ((1,), (0,)))
                put(out, c, a, rows * scale[a] if gated_by else rows)
                return carry

            lax.fori_loop(0, GROUPS, group, 0)
            exchange(n, c, out, into)
            return carry

        lax.fori_loop(0, CHUNKS, chunk, 0)

    choose(0, x_own, x_send, x_recv, False)
    choose(1, d_own, d_send, d_recv, True)

    repeat = lax.broadcasted_iota(jnp.int32, (PEERS, ROWS), 1) // TILE
    repeat = jnp.where(repeat == lax.broadcasted_iota(jnp.int32, (PEERS, ROWS), 0), 1.0, 0.0)
    repeat = repeat.astype(BF16)
    codes = dot(code.astype(BF16), repeat, ((0,), (0,)))
    gates = dot(gate.astype(BF16), repeat, ((0,), (0,)))
    place_of = (lax.broadcasted_iota(jnp.int32, codes.shape, 1) % TILE).astype(F32)
    for a in range(GROUPS):
        hit = codes == place_of + F32(a * TILE)
        back[a] = jnp.where(hit, 1.0, 0.0).astype(BF16)
        gated[a] = jnp.where(hit, gates, 0.0).astype(BF16)

    get_wi.wait()
    get_wo.wait()
    for c in range(CHUNKS):
        await_bytes(x_recv.at[c], recv.at[0, c])

    def forward(a, carry):
        total = jnp.zeros((ROWS, 2 * hidden), F32)
        for c in range(CHUNKS):
            total += dot(flat(x_recv[c, a]), wi[pl.ds(c * wide, wide), :], ((1,), (0,)))
        pre[a] = total
        g, up = total[:, :hidden], total[:, hidden:]
        act[a] = (g * jax.nn.sigmoid(g) * up).astype(BF16)
        return carry

    lax.fori_loop(0, GROUPS, forward, 0)

    for c in range(CHUNKS):
        sent(0, c, x_send)

        def group(a, carry, c=c):
            put(x_send, c, a, dot(act[a], wo[:, pl.ds(c * wide, wide)], ((1,), (0,))))
            return carry

        lax.fori_loop(0, GROUPS, group, 0)
        exchange(2, c, x_send, o_recv)

    for c in range(CHUNKS):
        await_bytes(d_recv.at[c], recv.at[1, c])

    def backward(a, carry):
        d_act = jnp.zeros((ROWS, hidden), F32)
        for c in range(CHUNKS):
            d_act += dot(flat(d_recv[c, a]), wo[:, pl.ds(c * wide, wide)], ((1,), (1,)))
        both = pre[a]
        g, up = both[:, :hidden], both[:, hidden:]
        sig = jax.nn.sigmoid(g)
        d_pre[a, :, pl.ds(0, hidden)] = (d_act * up * sig * (1.0 + g * (1.0 - sig))).astype(BF16)
        d_pre[a, :, pl.ds(hidden, hidden)] = (d_act * (g * sig)).astype(BF16)
        return carry

    lax.fori_loop(0, GROUPS, backward, 0)

    for c in range(CHUNKS):
        sent(1, c, d_send)

        def group(a, carry, c=c):
            put(d_send, c, a, dot(d_pre[a], wi[pl.ds(c * wide, wide), :], ((1,), (1,))))
            return carry

        lax.fori_loop(0, GROUPS, group, 0)
        exchange(3, c, d_send, r_recv)

    copies = []
    for i in (1, 2, 3, 0):
        c = (dp + i) % CHUNKS
        slot = i % 2
        if i in (3, 0):
            for copy in copies[(i - 3) % 4]:
                copy.wait_send()

        def grad_i(a, total, c=c):
            return total + dot(flat(x_recv[c, a]), d_pre[a], ((0,), (0,)))

        def grad_o(a, total, c=c):
            return total + dot(act[a], flat(d_recv[c, a]), ((0,), (0,)))

        g_in[slot] = lax.fori_loop(0, GROUPS, grad_i, jnp.zeros(g_in.shape[1:], F32)).astype(BF16)
        g_out[slot] = lax.fori_loop(0, GROUPS, grad_o, jnp.zeros(g_out.shape[1:], F32)).astype(BF16)
        if i:
            pair = [
                remote(g_in.at[slot], grad_in.at[dp], gi_s.at[i], gi_r.at[i], (c, ex)),
                remote(g_out.at[slot], grad_out.at[dp], go_s.at[i], go_r.at[i], (c, ex)),
            ]
        else:
            pair = [
                pltpu.make_async_copy(g_in.at[slot], grad_in.at[dp], gi_s.at[i]),
                pltpu.make_async_copy(g_out.at[slot], grad_out.at[dp], go_s.at[i]),
            ]
        for copy in pair:
            copy.start()
        copies.append(pair)

    def gather(n, weights, came, own, parts):
        for c in range(CHUNKS):
            await_bytes(came.at[c], recv.at[n + 2, c])

            def group(a, total, c=c):
                return total + dot(weights[a], flat(came[c, a]), ((1,), (0,)))

            total = lax.fori_loop(0, GROUPS, group, jnp.zeros((RING * own.shape[2], wide), F32))
            await_bytes(own.at[c, pl.ds(0, RING - 1)], own_s.at[n, c])
            own[c] = total.reshape(RING, -1, wide).astype(BF16)
            for i in range(1, RING):
                other = (y + i) % RING
                remote(
                    own.at[c, other], parts.at[c, i - 1], part_s.at[n, c], part_r.at[n, c], ring_id(other)
                ).start()

    def finish(n, own, parts, out):
        for c in range(CHUNKS):
            await_bytes(parts.at[c], part_r.at[n, c])
            total = own[c, y].astype(F32)
            for i in range(RING - 1):
                total += parts[c, i].astype(F32)
            out[:, pl.ds(c * wide, wide)] = total.astype(BF16)

    gather(0, gated, o_recv, x_own, m_recv)
    gather(1, back, r_recv, d_own, t_recv)
    finish(0, x_own, m_recv, mixed)
    finish(1, d_own, t_recv, d_tokens)

    for c in range(CHUNKS):
        sent(2, c, x_send)
        sent(3, c, d_send)
        for n, own in ((0, x_own), (1, d_own)):
            await_bytes(own.at[c, pl.ds(0, RING - 1)], part_s.at[n, c])
    await_bytes(tabs.at[pl.ds(0, RING - 1)], tab_s)
    for copy in copies[2]:
        copy.wait_send()
    for copy in copies[3]:
        copy.wait()
    for pair in copies[:3]:
        for copy in pair:
            copy.wait_recv()


def body(tokens, d_mixed, w_in, w_out, expert_ids, gate_fixed, placement):
    tok_rows, width = tokens.shape
    hidden = w_out.shape[1]
    wide = width // CHUNKS
    experts = RING * PEERS
    gates = gate_fixed.astype(F32)
    gates = gates / jnp.sum(gates, axis=1, keepdims=True)
    catalog = jnp.arange(experts, dtype=jnp.int32)
    copy, holder = placement % RING, placement // RING
    home = ((copy // CORES) * 2 + holder // PLANE) * PEERS + (copy % CORES) * PLANE + holder % PLANE
    target = jnp.sum(jnp.where(expert_ids[:, :, None] == catalog, home, 0), axis=2)
    hits = target[:, :, None] == catalog
    sent = jnp.any(hits, axis=1)
    weight = jnp.sum(jnp.where(hits, gates[:, :, None], 0.0), axis=1)
    t_ids = jnp.arange(tok_rows, dtype=jnp.int32)
    before = (t_ids[:, None] > t_ids[None, :]).astype(BF16)
    rank = jnp.dot(before, sent.astype(BF16), preferred_element_type=F32)
    y = (lax.axis_index("dp") // CORES) * 2 + lax.axis_index("expert") // PLANE
    code = jnp.where(sent, rank * RING + y.astype(F32), -1.0)
    tables = jnp.stack([code.T, weight.T]).reshape(2, RING, PEERS, tok_rows).transpose(1, 0, 2, 3)

    shuttle = pltpu.VMEM((CHUNKS, GROUPS, PEERS, TILE, wide), BF16)
    own = pltpu.VMEM((CHUNKS, RING, tok_rows, wide), BF16)
    parts = pltpu.VMEM((CHUNKS, RING - 1, tok_rows, wide), BF16)
    dma = pltpu.SemaphoreType.DMA
    anywhere = pl.BlockSpec(memory_space=pl.ANY)
    inside = pl.BlockSpec(memory_space=pltpu.VMEM)
    all_tokens = RING * tok_rows
    return pl.pallas_call(
        kernel,
        out_shape=(
            jax.ShapeDtypeStruct((tok_rows, width), BF16),
            jax.ShapeDtypeStruct((tok_rows, width), BF16),
            jax.ShapeDtypeStruct((RING, wide, 2 * hidden), BF16),
            jax.ShapeDtypeStruct((RING, hidden, wide), BF16),
        ),
        in_specs=[anywhere] * 5,
        out_specs=(inside, inside, anywhere, anywhere),
        scratch_shapes=[
            own, own, shuttle, shuttle, shuttle, shuttle, shuttle, shuttle, parts, parts,
            pltpu.VMEM((RING, 2, PEERS, tok_rows), F32),
            pltpu.VMEM((width, 2 * hidden), BF16),
            pltpu.VMEM((hidden, width), BF16),
            pltpu.VMEM((GROUPS, ROWS, all_tokens), BF16),
            pltpu.VMEM((GROUPS, ROWS, 1), F32),
            pltpu.VMEM((GROUPS, all_tokens, ROWS), BF16),
            pltpu.VMEM((GROUPS, all_tokens, ROWS), BF16),
            pltpu.VMEM((GROUPS, ROWS, 2 * hidden), F32),
            pltpu.VMEM((GROUPS, ROWS, hidden), BF16),
            pltpu.VMEM((GROUPS, ROWS, 2 * hidden), BF16),
            pltpu.VMEM((2, wide, 2 * hidden), BF16),
            pltpu.VMEM((2, hidden, wide), BF16),
            dma((2,)), dma, dma, dma((2, CHUNKS)), dma((2, CHUNKS)),
            dma((4, CHUNKS)), dma((4, CHUNKS)), dma((2, CHUNKS)), dma((2, CHUNKS)),
            dma((4,)), dma((4,)), dma((4,)), dma((4,)),
        ],
        compiler_params=pltpu.CompilerParams(
            has_side_effects=True, vmem_limit_bytes=60 * 1024 * 1024
        ),
        cost_estimate=pl.CostEstimate(flops=36 * 10**9, bytes_accessed=30 * 10**6, transcendentals=10**6),
    )(tokens, d_mixed, tables, w_in, w_out)


def solution(mesh):
    in_specs = (
        P(ALL, None),
        P(ALL, None),
        P("expert", None, None),
        P("expert", None, None),
        P(ALL, None),
        P(ALL, None),
        P(),
    )
    out_specs = (P(ALL, None), P(ALL, None), P("expert", "dp", None), P("expert", None, "dp"))
    return jax.shard_map(body, mesh=mesh, in_specs=in_specs, out_specs=out_specs, check_vma=False)
```

time: 454 us -> 303 us (0.67)
  the two profiles are of different devices: /device:TPU:0 before, /device:TPU:4 now
where the time goes in v2:
time: 303 us
  Pallas kernels  287 us (95%)
  local copies, waits for them, and re-layouts  9.88 us (3%)
  other arithmetic  5.73 us (2%)
    pallas_call x1, Pallas kernels, body(): pl.pallas_call(kernel, out_shape=(jax.ShapeDtypeStruct((tok_rows, width),...  287 us
    unnamed x7, local copies, waits for them, and re-layouts  9.57 us

profile of v2, /device:TPU:4, one launch (start us, length us, event | category | flops | bytes accessed | tf_op | source)
XLA Modules:
  0.0 303.1 jit_solution(2054693101670475610)
XLA Ops:
  0.7 0.7 fusion.4
  1.3 0.7 convert_reduce_fusion
  2.0 0.7 convert_divide_fusion
  2.7 0.1 copy.15
  2.8 0.8 copy.13
  3.6 2.4 select_reduce_fusion.1
  6.0 0.3 select_reduce_fusion
  6.4 0.3 fusion.2
  6.6 0.1 copy.16
  6.7 0.1 copy.14
  6.8 0.2 fusion.1
  7.0 0.7 maximum_bitcast_fusion.tables
  7.7 286.6 %shard_map.102 = (bf16[128,2048]{1,0:T(8,128)(2,1)}, bf16[128,2048]{1,0:T(8,128)(2,1)}, bf16[4,512,768]{2,1,0:T(8,128)(2,1)}, bf16[4,384,512]{2,1,0:T(8,128)(2,1)}) custom-call(bf16[128,2048]{1,0:T(8,128)(2,1)} %tokens.1, bf16[128,2048]{1,0:T(8,128)(2,1)} %d_mixed.1, f32[4,2,32,128]{3,2,1,0:T(8,128)} %maximum_bitcast_fusion.tables, ...), custom_call_target="tpu_custom_call" | custom-call | flops 35999997952 | bytes 30000000 | tf_op jit(solution)/shard_map/pallas_call | solution.py:288
  294.3 1.9 copy.22
  296.2 1.9 copy.23
  298.1 0.0 copy-start
  298.1 3.9 %copy.24 = bf16[4,512,768]{2,1,0:T(8,128)(2,1)} copy(bf16[4,512,768]{2,1,0:T(8,128)(2,1)} %get-tuple-element.10) | data formatting | bytes 6291456
  301.9 0.0 copy-done
  301.9 1.1 copy.25
Async XLA Ops:
  298.1 3.9 %copy-start = (bf16[4,384,512]{2,1,0:T(8,128)(2,1)S(1)}, bf16[4,384,512]{2,1,0:T(8,128)(2,1)}, u32[]{:S(2)}) copy-start(bf16[4,384,512]{2,1,0:T(8,128)(2,1)} %get-tuple-element.11) | copy-start | bytes 4718596

commit v3 on v2

v3 whole, which is shorter than its diff:
```python
import jax
import jax.numpy as jnp
from jax import lax
from jax.experimental import pallas as pl
from jax.experimental.pallas import tpu as pltpu
from jax.sharding import PartitionSpec as P

CAP = 10
F32 = jnp.float32
BF16 = jnp.bfloat16
ALL = ("dp", "expert")
MESH = pl.DeviceIdType.MESH
RING, PLANE, CORES = 4, 16, 2
PEERS = PLANE * CORES
CHUNKS, GROUPS, TILE = 4, 5, 8
ROWS = PEERS * TILE
EXPERTS = RING * PEERS
ALONG = "yxzy"
BATCHES = ((0,), (1, 2, 3))
D_BATCHES = ((0, 1, 2, 3),)
RINGS = "yxz"


def dot(a, b, dims):
    return lax.dot_general(a, b, (dims, ((), ())), preferred_element_type=F32)


def times(a, b):
    return dot(a, b, ((1,), (0,)))


def flat(block):
    return block.reshape(ROWS, block.shape[-1])


def iota(shape, axis):
    return lax.broadcasted_iota(jnp.int32, shape, axis)


def ones_where(hit):
    return jnp.where(hit, 1.0, 0.0).astype(BF16)


def in_plane(ring, x, y, z, core):
    first, last = {"y": (x, z), "x": (y, z), "z": (x, y)}[ring]
    return core * PLANE + first * RING + last


def kernel(
    tokens, d_mixed, ids, fixed, placement, w_in, w_out,
    m_parts, t_parts, grad_in, grad_out,
    x_own, d_own, x_send, d_send, x_recv, d_recv, o_recv, r_recv,
    tables, tabs, wi, wo, pick, scale, order, back, gated, pre, act, d_pre, g_in, g_out,
    w_sem, tab_s, tab_r, own_s, own_r, send, recv, part_s, part_r, gi_s, gi_r, go_s, go_r,
):
    dp, ex = lax.axis_index("dp"), lax.axis_index("expert")
    core, y_hi, y_lo = dp % CORES, dp // CORES, ex // PLANE
    x, y, z = (ex // RING) % RING, y_hi * 2 + y_lo, ex % RING
    at = {"x": x, "y": y, "z": z}
    me = {ring: in_plane(ring, x, y, z, core) for ring in RINGS}
    wide = x_send.shape[-1]
    hidden = act.shape[-1]

    def device(x, y, z, core):
        return ((y // 2) * CORES + core, (y % 2) * PLANE + x * RING + z)

    def on_ring(ring, other):
        return device(**{**at, ring: other}, core=core)

    def remote(src, dst, s, r, device):
        return pltpu.make_async_remote_copy(
            src_ref=src, dst_ref=dst, send_sem=s, recv_sem=r, device_id=device, device_id_type=MESH
        )

    def await_bytes(ref, sem):
        pltpu.make_async_copy(ref, ref, sem).wait()

    get_wi = pltpu.make_async_copy(w_in.at[dp], wi, w_sem.at[0])
    get_wo = pltpu.make_async_copy(w_out.at[dp], wo, w_sem.at[1])

    def spread(n, rows, own):
        for c, ring in enumerate(ALONG):
            part = rows.at[:, pl.ds(c * wide, wide)]
            for i in range(1, RING):
                other = (at[ring] + i) % RING
                remote(
                    part, own.at[c, at[ring]], own_s.at[n, c], own_r.at[n, c], on_ring(ring, other)
                ).start()
            pltpu.make_async_copy(part, own.at[c, at[ring]], own_r.at[n, c]).start()

    spread(0, tokens, x_own)

    tok_rows = ids.shape[1]
    square = (EXPERTS, tok_rows)
    gates = fixed[...].astype(F32)
    gates = gates / jnp.sum(gates, axis=0, keepdims=True)
    routed = jnp.zeros(square, F32)
    weight = jnp.zeros(square, F32)
    for k in range(ids.shape[0]):
        hit = ids[pl.ds(k, 1), :] == iota(square, 0)
        routed += jnp.where(hit, 1.0, 0.0)
        weight += jnp.where(hit, gates[k : k + 1, :], 0.0)
    earlier = ones_where(iota((tok_rows, tok_rows), 0) < iota((tok_rows, tok_rows), 1))
    ranks = jnp.where(routed > 0.0, times(routed.astype(BF16), earlier) * RING + 1.0, 0.0).astype(BF16)
    high = weight.astype(BF16)
    middle = (weight - high.astype(F32)).astype(BF16)
    low = (weight - high.astype(F32) - middle.astype(F32)).astype(BF16)
    slot = placement[...]
    copy, holder = slot & 3, slot >> 2
    home = {"x": (holder >> 2) & 3, "y": (copy >> 1) * 2 + (holder >> 4), "z": holder & 3}
    for t, ring in enumerate(RINGS):
        target = home[ring] * PEERS + in_plane(ring, core=copy & 1, **home)
        move = ones_where(iota((EXPERTS, EXPERTS), 0) == target)
        code = times(move, ranks)
        code = jnp.where(code > 0.0, code - 1.0 + at[ring].astype(F32), -1.0)
        gate = times(move, high) + times(move, middle) + times(move, low)
        tables[t, :, 0] = code.reshape(RING, PEERS, tok_rows)
        tables[t, :, 1] = gate.reshape(RING, PEERS, tok_rows)
        for i in range(1, RING):
            other = (at[ring] + i) % RING
            remote(
                tables.at[t, other], tabs.at[t, at[ring]], tab_s.at[t], tab_r.at[t], on_ring(ring, other)
            ).start()
        pltpu.make_async_copy(tables.at[t, at[ring]], tabs.at[t, at[ring]], tab_r.at[t]).start()

    spread(1, d_mixed, d_own)
    get_wi.start()
    get_wo.start()

    def table(t, kind):
        return jnp.concatenate([tabs[t, s, kind] for s in range(RING)], axis=1)

    everyone = RING * tok_rows
    row = iota((PEERS, TILE, everyone), 1).astype(F32)

    def make_pick(t):
        await_bytes(tabs.at[t], tab_r.at[t])
        code = table(t, 0)
        for a in range(GROUPS):
            hit = code[:, None, :] == row + F32(a * TILE)
            pick[t, a] = flat(jnp.where(hit, 1.0, 0.0)).astype(BF16)

    def make_scale(t):
        code, gate = table(t, 0), table(t, 1)
        for a in range(GROUPS):
            hit = code[:, None, :] == row + F32(a * TILE)
            scale[t, a] = flat(jnp.sum(jnp.where(hit, gate[:, None, :], 0.0), axis=2, keepdims=True))

    def exchange(several):
        def one(i, carry):
            for n, c, ring, out, into in several:
                shift = dict(zip([r for r in "xyz" if r != ring], (i // RING, i)))
                there = {r: (at[r] + shift[r]) % RING if r in shift else at[r] for r in "xyz"}
                there["core"] = (core + i // PLANE) % CORES
                remote(
                    out.at[c, :, in_plane(ring, **there)],
                    into.at[c, :, me[ring]],
                    send.at[n, c],
                    recv.at[n, c],
                    device(**there),
                ).start()
            return carry

        lax.fori_loop(1, PEERS, one, 0)
        for n, c, ring, out, into in several:
            mine = me[ring]
            pltpu.make_async_copy(out.at[c, :, mine], into.at[c, :, mine], recv.at[n, c]).start()

    def sent(n, c, out):
        await_bytes(out.at[c, :, pl.ds(0, PEERS - 1)], send.at[n, c])

    def put(out, c, a, rows):
        out[c, a] = rows.reshape(PEERS, TILE, rows.shape[-1]).astype(BF16)

    def choose(n, c, own, out):
        t = RINGS.index(ALONG[c])
        await_bytes(own.at[c], own_r.at[n, c])

        def group(a, carry):
            rows = times(pick[t, a], own[c].reshape(-1, wide))
            put(out, c, a, rows * scale[t, a] if n else rows)
            return carry

        lax.fori_loop(0, GROUPS, group, 0)

    made = set()
    for batch in BATCHES:
        for c in batch:
            t = RINGS.index(ALONG[c])
            if t not in made:
                make_pick(t)
                made.add(t)
            choose(0, c, x_own, x_send)
        exchange([(0, c, ALONG[c], x_send, x_recv) for c in batch])
    for t in sorted(made):
        make_scale(t)
    for batch in D_BATCHES:
        for c in batch:
            choose(1, c, d_own, d_send)
        exchange([(1, c, ALONG[c], d_send, d_recv) for c in batch])

    to, source = iota((ROWS, ROWS), 0), iota((ROWS, ROWS), 1)
    parts = {"x": (to >> 5) & 3, "y": to & 3, "z": (to >> 3) & 3}
    for t, ring in enumerate(RINGS[1:]):
        at_row = in_plane(ring, core=to >> 7, **parts) * TILE + ((to >> 2) & 1) * RING + parts[ring]
        order[t] = ones_where(source == at_row)

    repeat = ones_where((iota((PEERS, ROWS), 1) >> 3) == iota((PEERS, ROWS), 0))
    codes = dot(table(0, 0).astype(BF16), repeat, ((0,), (0,)))
    shares = dot(table(0, 1).astype(BF16), repeat, ((0,), (0,)))
    within = (iota(codes.shape, 1) & (TILE - 1)).astype(F32)
    for a in range(GROUPS):
        hit = codes == within + F32(a * TILE)
        back[a] = ones_where(hit)
        gated[a] = jnp.where(hit, shares, 0.0).astype(BF16)

    def arrive(n, into):
        for c, ring in enumerate(ALONG):
            await_bytes(into.at[c], recv.at[n, c])
            if ring != "y":

                def group(a, carry, c=c, t=RINGS.index(ring) - 1):
                    put(into, c, a, times(order[t], flat(into[c, a])))
                    return carry

                lax.fori_loop(0, GROUPS, group, 0)

    get_wi.wait()
    get_wo.wait()
    arrive(0, x_recv)

    def forward(a, carry):
        total = jnp.zeros((ROWS, 2 * hidden), F32)
        for c in range(CHUNKS):
            total += dot(flat(x_recv[c, a]), wi[pl.ds(c * wide, wide), :], ((1,), (0,)))
        pre[a] = total
        g, up = total[:, :hidden], total[:, hidden:]
        act[a] = (g * jax.nn.sigmoid(g) * up).astype(BF16)
        return carry

    lax.fori_loop(0, GROUPS, forward, 0)

    for c in range(CHUNKS):
        sent(0, c, x_send)

        def group(a, carry, c=c):
            put(x_send, c, a, dot(act[a], wo[:, pl.ds(c * wide, wide)], ((1,), (0,))))
            return carry

        lax.fori_loop(0, GROUPS, group, 0)
        exchange([(2, c, "y", x_send, o_recv)])

    arrive(1, d_recv)

    def backward(a, carry):
        d_act = jnp.zeros((ROWS, hidden), F32)
        for c in range(CHUNKS):
            d_act += dot(flat(d_recv[c, a]), wo[:, pl.ds(c * wide, wide)], ((1,), (1,)))
        both = pre[a]
        g, up = both[:, :hidden], both[:, hidden:]
        sig = jax.nn.sigmoid(g)
        d_pre[a, :, pl.ds(0, hidden)] = (d_act * up * sig * (1.0 + g * (1.0 - sig))).astype(BF16)
        d_pre[a, :, pl.ds(hidden, hidden)] = (d_act * (g * sig)).astype(BF16)
        return carry

    lax.fori_loop(0, GROUPS, backward, 0)

    for c in range(CHUNKS):
        sent(1, c, d_send)

        def group(a, carry, c=c):
            put(d_send, c, a, dot(d_pre[a], wi[pl.ds(c * wide, wide), :], ((1,), (1,))))
            return carry

        lax.fori_loop(0, GROUPS, group, 0)
        exchange([(3, c, "y", d_send, r_recv)])

    copies = []
    for i in (1, 2, 3, 0):
        c = (dp + i) % CHUNKS
        slot = i % 2
        if i in (3, 0):
            for copy in copies[(i - 3) % 4]:
                copy.wait_send()

        def grad_i(a, total, c=c):
            return total + dot(flat(x_recv[c, a]), d_pre[a], ((0,), (0,)))

        def grad_o(a, total, c=c):
            return total + dot(act[a], flat(d_recv[c, a]), ((0,), (0,)))

        g_in[slot] = lax.fori_loop(0, GROUPS, grad_i, jnp.zeros(g_in.shape[1:], F32)).astype(BF16)
        g_out[slot] = lax.fori_loop(0, GROUPS, grad_o, jnp.zeros(g_out.shape[1:], F32)).astype(BF16)
        if i:
            pair = [
                remote(g_in.at[slot], grad_in.at[dp], gi_s.at[i], gi_r.at[i], (c, ex)),
                remote(g_out.at[slot], grad_out.at[dp], go_s.at[i], go_r.at[i], (c, ex)),
            ]
        else:
            pair = [
                pltpu.make_async_copy(g_in.at[slot], grad_in.at[dp], gi_s.at[i]),
                pltpu.make_async_copy(g_out.at[slot], grad_out.at[dp], go_s.at[i]),
            ]
        for copy in pair:
            copy.start()
        copies.append(pair)

    def gather(n, weights, came, own, parts):
        for c in range(CHUNKS):
            await_bytes(came.at[c], recv.at[n + 2, c])

            def group(a, total, c=c):
                return total + times(weights[a], flat(came[c, a]))

            total = lax.fori_loop(0, GROUPS, group, jnp.zeros((everyone, wide), F32))
            await_bytes(own.at[c, pl.ds(0, RING - 1)], own_s.at[n, c])
            own[c] = total.reshape(RING, -1, wide).astype(BF16)
            for i in range(1, RING):
                other = (y + i) % RING
                remote(
                    own.at[c, other], parts.at[c, y], part_s.at[n, c], part_r.at[n, c], on_ring("y", other)
                ).start()
            pltpu.make_async_copy(own.at[c, y], parts.at[c, y], part_r.at[n, c]).start()

    gather(0, gated, o_recv, x_own, m_parts)
    gather(1, back, r_recv, d_own, t_parts)
    for c in range(CHUNKS):
        sent(2, c, x_send)
        sent(3, c, d_send)
        for n, own in ((0, x_own), (1, d_own)):
            await_bytes(own.at[c, pl.ds(0, RING - 1)], part_s.at[n, c])
    for t in range(len(RINGS)):
        await_bytes(tabs.at[t, pl.ds(0, RING - 1)], tab_s.at[t])
    for copy in copies[2]:
        copy.wait_send()
    for copy in copies[3]:
        copy.wait()
    for pair in copies[:3]:
        for copy in pair:
            copy.wait_recv()
    for c in range(CHUNKS):
        await_bytes(m_parts.at[c], part_r.at[0, c])
        await_bytes(t_parts.at[c], part_r.at[1, c])


def finish(
    m_parts, t_parts, from_in, from_out, mixed, d_tokens, grad_in, grad_out,
    m_held, t_held, in_held, out_held, got, grad_got, gone,
):
    gets = [
        [
            pltpu.make_async_copy(parts.at[c], into.at[c], got.at[n, c])
            for n, (parts, into) in enumerate(((m_parts, m_held), (t_parts, t_held)))
        ]
        for c in range(CHUNKS)
    ]
    through = [
        (
            pltpu.make_async_copy(source.at[e], held.at[e], grad_got.at[n, e]),
            pltpu.make_async_copy(held.at[e], to.at[e], gone.at[n, e]),
        )
        for e in range(RING)
        for n, (source, held, to) in enumerate(
            ((from_in, in_held, grad_in), (from_out, out_held, grad_out))
        )
    ]
    for get, _ in through:
        get.start()
    for pair in gets:
        for get in pair:
            get.start()
    for get, leave in through:
        get.wait()
        leave.start()
    wide = m_parts.shape[-1]
    for c in range(CHUNKS):
        for get, parts, out in zip(gets[c], (m_held, t_held), (mixed, d_tokens)):
            get.wait()
            total = parts[c, 0].astype(F32)
            for s in range(1, RING):
                total += parts[c, s].astype(F32)
            out[:, pl.ds(c * wide, wide)] = total.astype(BF16)
    for _, leave in through:
        leave.wait()


def body(tokens, d_mixed, w_in, w_out, expert_ids, gate_fixed, placement):
    tok_rows, width = tokens.shape
    hidden = w_out.shape[1]
    wide = width // CHUNKS
    shuttle = pltpu.VMEM((CHUNKS, GROUPS, PEERS, TILE, wide), BF16)
    own = pltpu.VMEM((CHUNKS, RING, tok_rows, wide), BF16)
    dma = pltpu.SemaphoreType.DMA
    anywhere = pl.BlockSpec(memory_space=pl.ANY)
    inside = pl.BlockSpec(memory_space=pltpu.VMEM)
    everyone = RING * tok_rows
    kinds = len(RINGS)
    whole = jax.ShapeDtypeStruct((tok_rows, width), BF16)
    part = jax.ShapeDtypeStruct((CHUNKS, RING, tok_rows, wide), BF16)
    grads = (
        jax.ShapeDtypeStruct((RING, wide, 2 * hidden), BF16),
        jax.ShapeDtypeStruct((RING, hidden, wide), BF16),
    )
    found = pl.pallas_call(
        kernel,
        out_shape=(part, part, *grads),
        in_specs=[anywhere, anywhere, inside, inside, inside, anywhere, anywhere],
        out_specs=[anywhere] * 4,
        scratch_shapes=[
            own, own, shuttle, shuttle, shuttle, shuttle, shuttle, shuttle,
            pltpu.VMEM((kinds, RING, 2, PEERS, tok_rows), F32),
            pltpu.VMEM((kinds, RING, 2, PEERS, tok_rows), F32),
            pltpu.VMEM((width, 2 * hidden), BF16),
            pltpu.VMEM((hidden, width), BF16),
            pltpu.VMEM((kinds, GROUPS, ROWS, everyone), BF16),
            pltpu.VMEM((kinds, GROUPS, ROWS, 1), F32),
            pltpu.VMEM((max(kinds - 1, 1), ROWS, ROWS), BF16),
            pltpu.VMEM((GROUPS, everyone, ROWS), BF16),
            pltpu.VMEM((GROUPS, everyone, ROWS), BF16),
            pltpu.VMEM((GROUPS, ROWS, 2 * hidden), F32),
            pltpu.VMEM((GROUPS, ROWS, hidden), BF16),
            pltpu.VMEM((GROUPS, ROWS, 2 * hidden), BF16),
            pltpu.VMEM((2, wide, 2 * hidden), BF16),
            pltpu.VMEM((2, hidden, wide), BF16),
            dma((2,)), dma((kinds,)), dma((kinds,)), dma((2, CHUNKS)), dma((2, CHUNKS)),
            dma((4, CHUNKS)), dma((4, CHUNKS)), dma((2, CHUNKS)), dma((2, CHUNKS)),
            dma((4,)), dma((4,)), dma((4,)), dma((4,)),
        ],
        compiler_params=pltpu.CompilerParams(
            has_side_effects=True, vmem_limit_bytes=60 * 1024 * 1024
        ),
        cost_estimate=pl.CostEstimate(flops=36 * 10**9, bytes_accessed=30 * 10**6, transcendentals=10**6),
    )(tokens, d_mixed, expert_ids.T, gate_fixed.T, placement.reshape(1, -1), w_in, w_out)
    return pl.pallas_call(
        finish,
        out_shape=(whole, whole, *grads),
        in_specs=[anywhere] * 4,
        out_specs=(inside, inside, anywhere, anywhere),
        scratch_shapes=[
            *[pltpu.VMEM(held.shape, BF16) for held in (part, part, *grads)],
            dma((2, CHUNKS)), dma((2, RING)), dma((2, RING)),
        ],
        compiler_params=pltpu.CompilerParams(vmem_limit_bytes=60 * 1024 * 1024),
    )(*found)


def solution(mesh):
    in_specs = (
        P(ALL, None),
        P(ALL, None),
        P("expert", None, None),
        P("expert", None, None),
        P(ALL, None),
        P(ALL, None),
        P(),
    )
    out_specs = (P(ALL, None), P(ALL, None), P("expert", "dp", None), P("expert", None, "dp"))
    return jax.shard_map(body, mesh=mesh, in_specs=in_specs, out_specs=out_specs, check_vma=False)
```

time: 303 us -> 251 us (0.83)
  the two profiles are of different devices: /device:TPU:4 before, /device:TPU:0 now
where the time goes in v3:
time: 251 us; the launch traced here: 249 us
  Pallas kernels  249 us (99%)
    pallas_call x1, Pallas kernels, body(): pl.pallas_call(kernel, out_shape=(part, part, *grads), in_specs=[anywhere...  242 us
    pallas_call x1, Pallas kernels, body(): pl.pallas_call(finish, out_shape=(whole, whole, *grads), in_specs=[anywhe...  6.16 us

profile of v3, /device:TPU:0, one launch (start us, length us, event | category | flops | bytes accessed | tf_op | source)
XLA Modules:
  0.0 249.5 jit_solution(1589234033847905355)
XLA Ops:
  0.6 242.5 %shard_map.102 = (bf16[4,4,128,512]{3,2,1,0:T(8,128)(2,1)}, bf16[4,4,128,512]{3,2,1,0:T(8,128)(2,1)}, bf16[4,512,768]{2,1,0:T(8,128)(2,1)}, bf16[4,384,512]{2,1,0:T(8,128)(2,1)}) custom-call(bf16[128,2048]{1,0:T(8,128)(2,1)} %tokens.1, bf16[128,2048]{1,0:T(8,128)(2,1)} %d_mixed.1, s32[8,128]{1,0:T(8,128)} %bitcast.3, s32[8,128]{1,0:T(8,128)} %bitcast.4, ...), custom_call_target="tpu_custom_call" | custom-call | flops 35999997952 | bytes 30000000 | tf_op jit(solution)/shard_map/pallas_call | solution.py:404
  243.1 6.2 %shard_map.103 = (bf16[128,2048]{1,0:T(8,128)(2,1)}, bf16[128,2048]{1,0:T(8,128)(2,1)}, bf16[4,512,768]{2,1,0:T(8,128)(2,1)}, bf16[4,384,512]{2,1,0:T(8,128)(2,1)}) custom-call(bf16[4,4,128,512]{3,2,1,0:T(8,128)(2,1)} %get-tuple-element.8.m_parts, bf16[4,4,128,512]{3,2,1,0:T(8,128)(2,1)} %get-tuple-element.9.t_parts, ...), custom_call_target="tpu_custom_call" | custom-call | tf_op jit(solution)/shard_map/pallas_call | solution.py:434

commit v4 on v3

--- a/solution.py
+++ b/solution.py
@@ -78,8 +78,9 @@
     get_wi = pltpu.make_async_copy(w_in.at[dp], wi, w_sem.at[0])
     get_wo = pltpu.make_async_copy(w_out.at[dp], wo, w_sem.at[1])
 
-    def spread(n, rows, own):
-        for c, ring in enumerate(ALONG):
+    def spread(n, rows, own, chunks):
+        for c in chunks:
+            ring = ALONG[c]
             part = rows.at[:, pl.ds(c * wide, wide)]
             for i in range(1, RING):
                 other = (at[ring] + i) % RING
@@ -88,7 +89,7 @@
                 ).start()
             pltpu.make_async_copy(part, own.at[c, at[ring]], own_r.at[n, c]).start()
 
-    spread(0, tokens, x_own)
+    spread(0, tokens, x_own, range(1))
 
     tok_rows = ids.shape[1]
     square = (EXPERTS, tok_rows)
@@ -123,7 +124,7 @@
             ).start()
         pltpu.make_async_copy(tables.at[t, at[ring]], tabs.at[t, at[ring]], tab_r.at[t]).start()
 
-    spread(1, d_mixed, d_own)
+    spread(0, tokens, x_own, range(1, CHUNKS))
     get_wi.start()
     get_wo.start()
 
@@ -192,6 +193,8 @@
                 made.add(t)
             choose(0, c, x_own, x_send)
         exchange([(0, c, ALONG[c], x_send, x_recv) for c in batch])
+        if batch is BATCHES[0]:
+            spread(1, d_mixed, d_own, range(CHUNKS))
     for t in sorted(made):
         make_scale(t)
     for batch in D_BATCHES:
@@ -364,11 +367,11 @@
             ((from_in, in_held, grad_in), (from_out, out_held, grad_out))
         )
     ]
-    for get, _ in through:
-        get.start()
     for pair in gets:
         for get in pair:
             get.start()
+    for get, _ in through:
+        get.start()
     for get, leave in through:
         get.wait()
         leave.start()

time: 251 us -> 251 us (level)
  no operation moved by 1% of the time
where the time goes in v4:
time: 251 us; the launch traced here: 249 us
  Pallas kernels  248 us (99%)
    pallas_call x1, Pallas kernels, body(): pl.pallas_call(kernel, out_shape=(part, part, *grads), in_specs=[anywhere...  242 us
    pallas_call x1, Pallas kernels, body(): pl.pallas_call(finish, out_shape=(whole, whole, *grads), in_specs=[anywhe...  6.31 us

profile of v4, /device:TPU:0, one launch (start us, length us, event | category | flops | bytes accessed | tf_op | source)
XLA Modules:
  0.0 249.0 jit_solution(4828880099100154372)
XLA Ops:
  0.6 241.9 %shard_map.102 = (bf16[4,4,128,512]{3,2,1,0:T(8,128)(2,1)}, bf16[4,4,128,512]{3,2,1,0:T(8,128)(2,1)}, bf16[4,512,768]{2,1,0:T(8,128)(2,1)}, bf16[4,384,512]{2,1,0:T(8,128)(2,1)}) custom-call(bf16[128,2048]{1,0:T(8,128)(2,1)} %tokens.1, bf16[128,2048]{1,0:T(8,128)(2,1)} %d_mixed.1, s32[8,128]{1,0:T(8,128)} %bitcast.3, s32[8,128]{1,0:T(8,128)} %bitcast.4, ...), custom_call_target="tpu_custom_call" | custom-call | flops 35999997952 | bytes 30000000 | tf_op jit(solution)/shard_map/pallas_call | solution.py:407
  242.6 6.3 %shard_map.103 = (bf16[128,2048]{1,0:T(8,128)(2,1)}, bf16[128,2048]{1,0:T(8,128)(2,1)}, bf16[4,512,768]{2,1,0:T(8,128)(2,1)}, bf16[4,384,512]{2,1,0:T(8,128)(2,1)}) custom-call(bf16[4,4,128,512]{3,2,1,0:T(8,128)(2,1)} %get-tuple-element.8.m_parts, bf16[4,4,128,512]{3,2,1,0:T(8,128)(2,1)} %get-tuple-element.9.t_parts, ...), custom_call_target="tpu_custom_call" | custom-call | tf_op jit(solution)/shard_map/pallas_call | solution.py:437
